TPU v7x, 32 devices: a whole 2x2x4 slice. The times are simulated.
32 devices in a mesh: wide: 8 (over z, x), narrow: 4 (over y, core).
Axes of the slice: x: 2, y: 2, z: 4, core: 2. Of those that a mesh axis runs over, the one named last changes fastest.
Arguments:
- tokens: bfloat16 [64, 512, 512], P(('wide', 'narrow')), may hold values from -6 to 6
- segment_ids: int32 [64, 512], P(('wide', 'narrow')), may hold values from 0 to 3, never falling along the last dimension, each value on 1 to 256 neighbouring positions
- matrices: bfloat16 [2, 5120, 512], P(None, ('wide', 'narrow')), may hold values from -1.5 to 1.5, as said below
- vectors: bfloat16 [2, 2560], replicated, may hold values from 0.5 to 1.5
- cotangent: bfloat16 [64, 512, 512], P(('wide', 'narrow')), may hold values from -6 to 6
Outputs:
- outputs: float32 [64, 512, 512], P(('wide', 'narrow'))
- input_grad: float32 [64, 512, 512], P(('wide', 'narrow'))
- matrix_grads: float32 [2, 5120, 512], P(None, ('wide', 'narrow'))
- vector_grads: float32 [2, 2560], replicated
Inputs may be any that keep to these rules, and one draw needn't show every extreme that they name: `segment_ids`: in each row the document numbers start at 0 and never fall; no document is longer than half of 512 positions. `matrices`: matrix entries are symmetric about zero.
All inputs are finite; a program needn't handle non-finite values.
Results may differ from a plain program's by a relative error of at most 0.0095.
Values may be sent and summed in bfloat16 or wider, within the bound.
A program may use at most 256 MiB of HBM per device.

v0:
```python
import jax
import jax.numpy as jnp
from jax import lax
from jax.sharding import PartitionSpec as P

D = 512
FF = 3072
S = 512
LAYERS = 2


EPSILON = 1e-05


def layer_norm(values, gain):
    center = values - jnp.mean(values, axis=-1, keepdims=True)
    spread = jnp.mean(center * center, axis=-1, keepdims=True)
    return center * lax.rsqrt(spread + EPSILON) * gain


def split_weights(mats, vecs):
    half_width = FF // 2
    return (
        mats[:FF],
        mats[FF : FF + half_width],
        mats[FF + half_width :],
        vecs[:D].astype(jnp.float32),
        vecs[D : D + half_width].astype(jnp.float32),
        vecs[D + half_width :].astype(jnp.float32),
    )


def forward_parts(inputs, weights, same):
    w_in_t, w_out, w_spatial, gain_in, gain_mid, bias_spatial = weights
    count = inputs.shape[0]
    half_width = FF // 2
    normed = layer_norm(inputs.reshape(-1, D), gain_in).astype(jnp.bfloat16)
    hidden_pre = jnp.einsum("td,fd->tf", normed, w_in_t, preferred_element_type=jnp.float32)
    hidden = jax.nn.gelu(hidden_pre)
    spatial_in = layer_norm(hidden[:, half_width:], gain_mid).astype(jnp.bfloat16)
    spatial_in = spatial_in.reshape(count, S, half_width)
    masked = jnp.where(same, w_spatial[None], jnp.zeros((), jnp.bfloat16))
    mixed = jnp.einsum("rij,rjc->ric", masked, spatial_in, preferred_element_type=jnp.float32)
    mixed = (mixed + bias_spatial[None, :, None]).reshape(-1, half_width)
    product = (hidden[:, :half_width] * mixed).astype(jnp.bfloat16)
    return (normed, hidden_pre, hidden, spatial_in, masked, mixed, product)


def backward_layer(inputs, weights, same, grad_out):
    w_in_t, w_out, w_spatial, gain_in, gain_mid, bias_spatial = weights
    count = inputs.shape[0]
    half_width = FF // 2
    normed, hidden_pre, hidden, spatial_in, masked, mixed, product = forward_parts(
        inputs, weights, same
    )
    grad_branch = grad_out.reshape(-1, D).astype(jnp.bfloat16)
    grad_w_out = jnp.einsum("tc,td->cd", product, grad_branch, preferred_element_type=jnp.float32)
    grad_product = jnp.einsum("td,cd->tc", grad_branch, w_out, preferred_element_type=jnp.float32)
    grad_gate = grad_product * mixed
    grad_mixed = (
        (grad_product * hidden[:, :half_width]).astype(jnp.bfloat16).reshape(count, S, half_width)
    )
    grad_bias = jnp.sum(grad_mixed.astype(jnp.float32), axis=(0, 2))
    outer = jnp.einsum("ric,rjc->rij", grad_mixed, spatial_in, preferred_element_type=jnp.float32)
    grad_spatial = jnp.sum(jnp.where(same, outer, 0.0), axis=0)
    grad_spatial_in = jnp.einsum(
        "rij,ric->rjc", masked, grad_mixed, preferred_element_type=jnp.float32
    )
    unused, pull_mid = jax.vjp(layer_norm, hidden[:, half_width:], gain_mid)
    grad_value, grad_gain_mid = pull_mid(grad_spatial_in.reshape(-1, half_width))
    unused, pull_gelu = jax.vjp(jax.nn.gelu, hidden_pre)
    grad_pre = pull_gelu(jnp.concatenate([grad_gate, grad_value], axis=1))[0].astype(jnp.bfloat16)
    grad_w_in_t = jnp.einsum("tf,td->fd", grad_pre, normed, preferred_element_type=jnp.float32)
    grad_normed = jnp.einsum("tf,fd->td", grad_pre, w_in_t, preferred_element_type=jnp.float32)
    unused, pull_in = jax.vjp(layer_norm, inputs.reshape(-1, D), gain_in)
    grad_inputs, grad_gain_in = pull_in(grad_normed)
    grad_inputs = grad_out + grad_inputs.reshape(inputs.shape)
    mat_grad = jnp.concatenate([grad_w_in_t, grad_w_out, grad_spatial], axis=0)
    vec_grad = jnp.concatenate([grad_gain_in, grad_gain_mid, grad_bias])
    return (grad_inputs, mat_grad, vec_grad)


def per_device(tokens, segment_ids, matrices, vectors, cotangent):
    same = segment_ids[:, :, None] == segment_ids[:, None, :]
    current = tokens.astype(jnp.float32)
    kept_inputs = []
    kept_weights = []
    for layer_index in range(LAYERS):
        gathered = lax.all_gather(matrices[layer_index], ("wide", "narrow"), axis=0, tiled=True)
        weights = split_weights(gathered, vectors[layer_index])
        kept_inputs.append(current)
        kept_weights.append(weights)
        parts = forward_parts(current, weights, same)
        branch = jnp.dot(parts[-1], weights[1], preferred_element_type=jnp.float32)
        current = current + branch.reshape(current.shape)
    grad_current = cotangent.astype(jnp.float32)
    mat_list = [None] * LAYERS
    vec_list = [None] * LAYERS
    for layer_index in reversed(range(LAYERS)):
        gathered = lax.all_gather(matrices[layer_index], ("wide", "narrow"), axis=0, tiled=True)
        weights = split_weights(gathered, vectors[layer_index])
        grad_current, mat_grad, vec_grad = backward_layer(
            kept_inputs[layer_index], weights, same, grad_current
        )
        vec_list[layer_index] = vec_grad
        mat_list[layer_index] = lax.psum_scatter(
            mat_grad, ("wide", "narrow"), scatter_dimension=0, tiled=True
        )[None]
    stacked = jnp.concatenate(mat_list, axis=0)
    vec_total = lax.psum(jnp.stack(vec_list), ("wide", "narrow"))
    return (current, grad_current, stacked, vec_total)


def solution(mesh):
    placed = (
        P(("wide", "narrow"), None, None),
        P(("wide", "narrow"), None),
        P(None, ("wide", "narrow"), None),
        P(),
        P(("wide", "narrow"), None, None),
    )
    return jax.shard_map(
        per_device,
        mesh=mesh,
        in_specs=placed,
        out_specs=(
            P(("wide", "narrow"), None, None),
            P(("wide", "narrow"), None, None),
            P(None, ("wide", "narrow"), None),
            P(),
        ),
        check_vma=False,
    )
```

profile of v0, /device:TPU:0, one launch (start us, length us, event | category | flops | bytes accessed | tf_op | source)
XLA Modules:
  0.0 542.7 jit_solution(10152717450321905773)
XLA Ops:
  16.2 63.2 %all-gather.5.cloned.1.call-done = bf16[1,5120,512]{2,1,0:T(8,128)(2,1)} async-done(((bf16[1,160,512]{2,1,0:T(8,128)(2,1)}), bf16[1,5120,512]{2,1,0:T(8,128)(2,1)}) %all-gather.5.cloned.1.call-update) | async-done | bytes 5242896 | tf_op jit(solution)/shard_map/all_gather | solution.py:89
  79.4 9.8 %multiply_multiply_fusion.5 = (f32[1024,3072]{1,0:T(8,128)S(1)}, f32[1024,3072]{1,0:T(8,128)}) fusion(bf16[1024,512]{1,0:T(8,128)(2,1)S(1)} %multiply_convert_fusion.5, bf16[1,5120,512]{2,1,0:T(8,128)(2,1)} %all-gather.5.cloned.1.call-done), kind=kOutput, calls=%fused_computation.21 | convolution fusion | flops 3246391296 | bytes 29360128 | tf_op jit(solution)/shard_map/td,fd->tf/dot_general | solution.py:38
  97.1 3.8 fusion.17
  100.9 4.2 fusion.27
  106.3 40.8 %all-gather.7.cloned.1.call-done = bf16[1,5120,512]{2,1,0:T(8,128)(2,1)} async-done(((bf16[1,160,512]{2,1,0:T(8,128)(2,1)}), bf16[1,5120,512]{2,1,0:T(8,128)(2,1)}) %all-gather.7.cloned.1.call-update) | async-done | bytes 5242896 | tf_op jit(solution)/shard_map/all_gather | solution.py:89
  147.0 9.8 %multiply_multiply_fusion.4 = (f32[1024,3072]{1,0:T(8,128)S(1)}, f32[1024,3072]{1,0:T(8,128)}) fusion(bf16[1024,512]{1,0:T(8,128)(2,1)S(1)} %multiply_convert_fusion.4, bf16[1,5120,512]{2,1,0:T(8,128)(2,1)} %all-gather.7.cloned.1.call-done), kind=kOutput, calls=%fused_computation.20 | convolution fusion | flops 3246391296 | bytes 29360128 | tf_op jit(solution)/shard_map/td,fd->tf/dot_general | solution.py:38
  158.8 7.1 %convert_reduce_fusion = (f32[1024]{0:T(1024)S(1)}, bf16[1024,1536]{1,0:T(8,128)(2,1)S(1)}, f32[1024]{0:T(1024)S(1)}, f32[1024,1536]{1,0:T(8,128)}) fusion(f32[1024,3072]{1,0:T(8,128)S(1)} %get-tuple-element.43, f32[1024]{0:T(1024)S(1)} %broadcast_multiply_fusion, bf16[1024,512]{1,0:T(8,128)(2,1)S(1)} %bitcast.149, ...), kind=kOutput, calls=%fused_computation.38 | convolution fusion | flops 1621620736 | bytes 24653824 | tf_op jit(solution)/shard_map/td,cd->tc/dot_general | solution.py:58
  172.4 4.3 fusion.59
  176.7 4.9 fusion.23
  181.7 4.6 convolution_add_fusion
  189.3 11.9 %bitcast_multiply_fusion.4 = (f32[1024,1536]{1,0:T(8,128)}, bf16[1024,1536]{1,0:T(8,128)(2,1)}) fusion(f32[1024,1536]{1,0:T(8,128)} %get-tuple-element.45, f32[2,512,1536]{2,1,0:T(8,128)} %convolution_add_fusion, f32[1024,3072]{1,0:T(8,128)} %copy-done.1), kind=kLoop, calls=%fused_computation.32 | loop fusion | flops 4718592 | bytes 28311552 | tf_op jit(solution)/shard_map/mul | solution.py:59
  201.2 12.4 %fusion.13 = bf16[1024,3072]{1,0:T(8,128)(2,1)S(1)} fusion(f32[1024,3072]{1,0:T(8,128)} %get-tuple-element.44, f32[1024,1536]{1,0:T(8,128)} %broadcast_add_fusion.1, f32[1024,1536]{1,0:T(8,128)} %get-tuple-element.29), kind=kLoop, calls=%fused_computation.17 | loop fusion | flops 66060288 | bytes 31457280 | tf_op jit(solution)/shard_map/convert_element_type | solution.py:72
  219.7 9.4 %pad_maximum_fusion.3 = f32[5120,512]{1,0:T(8,128)} fusion(f32[512,512]{1,0:T(8,128)S(1)} %copy-done.21, f32[1536,512]{1,0:T(8,128)S(1)} %fusion.65, f32[3072,512]{1,0:T(8,128)S(1)} %fusion.64), kind=kLoop, calls=%fused_computation.23 | loop fusion | flops 5242880 | bytes 20971520 | tf_op jit(solution)/shard_map/concatenate | solution.py:78
  229.2 7.4 %multiply_reduce_fusion.4 = (f32[512]{0:T(512)S(1)}, f32[1024]{0:T(1024)S(1)}, f32[1024,512]{1,0:T(8,128)S(1)}) fusion(f32[2,512,512]{2,1,0:T(8,128)S(1)} %get-tuple-element.25, f32[1024]{0:T(1024)S(1)} %rsqrt.50, f32[1024]{0:T(1024)S(1)} %bitcast.171, f32[512]{0:T(512)S(1)} %bitcast.178, bf16[1024,3072]{1,0:T(8,128)(2,1)} %copy-done.12, ...), kind=kOutput, calls=%fused_computation.72 | convolution fusion | flops 3224893952 | bytes 13647872 | tf_op jit(solution)/shard_map/tf,fd->td/dot_general | solution.py:74
  239.4 7.9 %convert_reduce_fusion.1 = (f32[1024]{0:T(1024)S(1)}, bf16[1024,1536]{1,0:T(8,128)(2,1)S(1)}, f32[1024,1536]{1,0:T(8,128)}) fusion(f32[1024,3072]{1,0:T(8,128)S(1)} %bitcast.140, f32[2,512,1536]{2,1,0:T(8,128)} %copy-done.4, bf16[1024,512]{1,0:T(8,128)(2,1)S(1)} %bitcast.152, bf16[1,5120,512]{2,1,0:T(8,128)(2,1)} %all-gather.5.cloned.1.call-done), kind=kOutput, calls=%fused_computation.39 | convolution fusion | flops 1618476032 | bytes 24645632 | tf_op jit(solution)/shard_map/td,cd->tc/dot_general | solution.py:58
  254.9 3.7 fusion.63
  262.1 10.4 %fusion.6 = bf16[1024,3072]{1,0:T(8,128)(2,1)S(1)} fusion(f32[1024,3072]{1,0:T(8,128)} %get-tuple-element.42, f32[1024,1536]{1,0:T(8,128)S(1)} %broadcast_add_fusion, f32[1024,1536]{1,0:T(8,128)S(1)} %bitcast.142), kind=kLoop, calls=%fused_computation.10 | loop fusion | flops 66060288 | bytes 31457280 | tf_op jit(solution)/shard_map/convert_element_type | solution.py:72
  272.6 3.6 fusion.62
  276.7 9.7 %pad_maximum_fusion.2 = f32[5120,512]{1,0:T(8,128)} fusion(f32[512,512]{1,0:T(8,128)S(1)} %fusion.22, f32[1536,512]{1,0:T(8,128)S(1)} %copy-done.16, f32[3072,512]{1,0:T(8,128)S(1)} %fusion.62), kind=kLoop, calls=%fused_computation.22 | loop fusion | flops 5242880 | bytes 20971520 | tf_op jit(solution)/shard_map/concatenate | solution.py:78
  286.6 4.3 fusion.29
  292.7 6.8 %multiply_reduce_fusion.6 = (f32[1024]{0:T(1024)S(1)}, f32[1024,512]{1,0:T(8,128)S(1)}) fusion(bf16[2,512,512]{2,1,0:T(8,128)(2,1)S(1)} %copy-done.3, f32[512]{0:T(512)S(1)} %bitcast.174, f32[1024]{0:T(1024)S(1)} %bitcast.163, bf16[1024,3072]{1,0:T(8,128)(2,1)} %copy-done.11, bf16[1,5120,512]{2,1,0:T(8,128)(2,1)} %all-gather.5.cloned.1.call-done), kind=kOutput, calls=%fused_computation.74 | convolution fusion | flops 3223845888 | bytes 12593152 | tf_op jit(solution)/shard_map/tf,fd->td/dot_general | solution.py:74
  302.1 42.2 %psum.7 = f32[2,2560]{1,0:T(2,128)} all-reduce(f32[2,2560]{1,0:T(2,128)S(1)} %pad_maximum_fusion.5), channel_id=1, replica_groups=mesh['wide'=8,'narrow'=4] {'wide','narrow'}, use_global_device_ids=true, to_apply=%region_28.29 | all-reduce | flops 5120 | bytes 40960 | tf_op jit(solution)/shard_map/psum | solution.py:110
  349.8 31.4 %reduce-scatter.5.cloned.1.call-done = f32[160,512]{1,0:T(8,128)} async-done(((f32[5120,512]{1,0:T(8,128)}), f32[160,512]{1,0:T(8,128)}) %reduce-scatter.5.cloned.1.call-update) | async-done | bytes 327696 | tf_op jit(solution)/shard_map/reduce_scatter | solution.py:106
  381.3 152.5 %reduce-scatter.3.cloned.1.call-done = f32[160,512]{1,0:T(8,128)} async-done(((f32[5120,512]{1,0:T(8,128)}), f32[160,512]{1,0:T(8,128)}) %reduce-scatter.3.cloned.1.call-update) | async-done | bytes 327696 | tf_op jit(solution)/shard_map/reduce_scatter | solution.py:106
  (155 shorter events, 61.6 us)
Async XLA Ops:
  7.2 72.3 %all-gather.5.cloned.1.call-start = ((), (), s32[]{:S(2)}) async-start(), calls=%async_computation.4 | async-start | bytes 5406720 | tf_op jit(solution)/shard_map/all_gather | solution.py:89
  9.0 138.1 %all-gather.7.cloned.1.call-start = ((), (), s32[]{:S(2)}) async-start(), calls=%async_computation.5 | async-start | bytes 5406720 | tf_op jit(solution)/shard_map/all_gather | solution.py:89
  9.7 371.5 %reduce-scatter.5.cloned.1.call-start = ((), (), s32[]{:S(2)}) async-start(), calls=%async_computation.3 | async-start | bytes 10813440 | tf_op jit(solution)/shard_map/reduce_scatter | solution.py:106
  11.2 78.0 %copy-start.27 = (f32[1,4,2,128]{3,1,2,0:T(4,128)}, f32[1,4,2,128]{3,1,2,0:T(4,128)S(1)}, u32[]{:S(2)}) copy-start(f32[1,4,2,128]{3,1,2,0:T(4,128)S(1)} %copy.15) | copy-start | bytes 12292
  12.9 76.3 %copy-start.31 = (f32[1,4,2,128]{3,1,2,0:T(4,128)}, f32[1,4,2,128]{3,1,2,0:T(4,128)S(1)}, u32[]{:S(2)}) copy-start(f32[1,4,2,128]{3,1,2,0:T(4,128)S(1)} %copy.16) | copy-start | bytes 12292
  13.0 76.2 %copy-start.29 = (f32[1024]{0:T(1024)}, f32[1024]{0:T(1024)S(1)}, u32[]{:S(2)}) copy-start(f32[1024]{0:T(1024)S(1)} %rsqrt.48) | copy-start | bytes 12292
  14.6 74.6 %copy-start.33 = (f32[1,512]{1,0:T(1,128)}, f32[1,512]{1,0:T(1,128)S(1)}, u32[]{:S(2)}) copy-start(f32[1,512]{1,0:T(1,128)S(1)} %get-tuple-element.36) | copy-start | bytes 6148
  16.2 73.0 %copy-start.22 = (bf16[1024,512]{1,0:T(8,128)(2,1)}, bf16[1024,512]{1,0:T(8,128)(2,1)S(1)}, u32[]{:S(2)}) copy-start(bf16[1024,512]{1,0:T(8,128)(2,1)S(1)} %multiply_convert_fusion.5) | copy-start | bytes 3145732
  89.2 7.9 %copy-start = (f32[1024,3072]{1,0:T(8,128)}, f32[1024,3072]{1,0:T(8,128)S(1)}, u32[]{:S(2)}) copy-start(f32[1024,3072]{1,0:T(8,128)S(1)} %get-tuple-element.41) | copy-start | bytes 37748740
  106.3 40.8 %copy-start.24 = (bf16[1024,512]{1,0:T(8,128)(2,1)}, bf16[1024,512]{1,0:T(8,128)(2,1)S(1)}, u32[]{:S(2)}) copy-start(bf16[1024,512]{1,0:T(8,128)(2,1)S(1)} %multiply_convert_fusion.4) | copy-start | bytes 3145732
  156.8 15.6 %copy-start.1 = (f32[1024,3072]{1,0:T(8,128)}, f32[1024,3072]{1,0:T(8,128)S(1)}, u32[]{:S(2)}) copy-start(f32[1024,3072]{1,0:T(8,128)S(1)} %get-tuple-element.43) | copy-start | bytes 37748740
  166.0 6.5 %copy-start.7 = (bf16[1024,1536]{1,0:T(8,128)(2,1)}, bf16[1024,1536]{1,0:T(8,128)(2,1)S(1)}, u32[]{:S(2)}) copy-start(bf16[1024,1536]{1,0:T(8,128)(2,1)S(1)} %get-tuple-element.17) | copy-start | bytes 9437188
  201.2 12.5 %copy-start.25 = (bf16[1024,512]{1,0:T(8,128)(2,1)S(1)}, bf16[1024,512]{1,0:T(8,128)(2,1)}, u32[]{:S(2)}) copy-start(bf16[1024,512]{1,0:T(8,128)(2,1)} %copy-done.24) | copy-start | bytes 3145732
  229.2 304.6 %reduce-scatter.3.cloned.1.call-start = ((), (), s32[]{:S(2)}) async-start(), calls=%async_computation.2 | async-start | bytes 10813440 | tf_op jit(solution)/shard_map/reduce_scatter | solution.py:106
  229.2 8.8 %slice-start = ((s8[12582912]{0:T(1024)(128)(4,1)}), s8[4194304]{0:T(1024)(128)(4,1)S(1)}, s32[]{:S(2)}) async-start(s8[12582912]{0:T(1024)(128)(4,1)} %bitcast.139), calls=%async_computation.6 | async-start | bytes 8388608
  229.2 8.8 %slice-start.1 = ((s8[12582912]{0:T(1024)(128)(4,1)}), s8[4194304]{0:T(1024)(128)(4,1)S(1)}, s32[]{:S(2)}) async-start(s8[12582912]{0:T(1024)(128)(4,1)} %bitcast.139), calls=%async_computation.7 | async-start | bytes 8388608
  237.7 9.6 %copy-start.5 = (f32[1024,512]{1,0:T(8,128)}, f32[1024,512]{1,0:T(8,128)S(1)}, u32[]{:S(2)}) copy-start(f32[1024,512]{1,0:T(8,128)S(1)} %broadcast_add_fusion.3) | copy-start | bytes 6291460
  239.4 7.9 %copy-start.14 = (bf16[512,512]{1,0:T(8,128)(2,1)S(1)}, bf16[512,512]{1,0:T(8,128)(2,1)}, u32[]{:S(2)}) copy-start(bf16[512,512]{1,0:T(8,128)(2,1)} %copy-done.13) | copy-start | bytes 1572868
  262.1 10.4 %copy-start.23 = (bf16[1024,512]{1,0:T(8,128)(2,1)S(1)}, bf16[1024,512]{1,0:T(8,128)(2,1)}, u32[]{:S(2)}) copy-start(bf16[1024,512]{1,0:T(8,128)(2,1)} %copy-done.22) | copy-start | bytes 3145732
  286.6 6.1 %copy-start.3 = (bf16[2,512,512]{2,1,0:T(8,128)(2,1)S(1)}, bf16[2,512,512]{2,1,0:T(8,128)(2,1)}, u32[]{:S(2)}) copy-start(bf16[2,512,512]{2,1,0:T(8,128)(2,1)} %param.5) | copy-start | bytes 3145732
  286.6 6.1 %copy-start.28 = (f32[1,4,2,128]{3,1,2,0:T(4,128)S(1)}, f32[1,4,2,128]{3,1,2,0:T(4,128)}, u32[]{:S(2)}) copy-start(f32[1,4,2,128]{3,1,2,0:T(4,128)} %copy-done.27) | copy-start | bytes 12292
  292.7 6.9 %copy-start.32 = (f32[1,4,2,128]{3,1,2,0:T(4,128)S(1)}, f32[1,4,2,128]{3,1,2,0:T(4,128)}, u32[]{:S(2)}) copy-start(f32[1,4,2,128]{3,1,2,0:T(4,128)} %copy-done.31) | copy-start | bytes 12292
  292.7 8.2 %copy-start.30 = (f32[1024]{0:T(1024)S(1)}, f32[1024]{0:T(1024)}, u32[]{:S(2)}) copy-start(f32[1024]{0:T(1024)} %copy-done.29) | copy-start | bytes 12292
  299.6 47.1 %copy-start.6 = (f32[1024,512]{1,0:T(8,128)S(1)}, f32[1024,512]{1,0:T(8,128)}, u32[]{:S(2)}) copy-start(f32[1024,512]{1,0:T(8,128)} %copy-done.5) | copy-start | bytes 6291460
  (20 other events, 65.9 us)
Sparse Core Ops, SparseCore 0:
  11.4 67.9 all-gather.4
  82.8 64.1 all-gather.6
  229.3 151.9 reduce-scatter.4
  383.4 150.3 reduce-scatter.2
where the time goes:
time: 553 us; the launch traced here: 543 us
  waiting for transfers between devices  289 us (52%)
  other arithmetic  95.9 us (17%)
  matrix products  87.2 us (16%)
  blocking collectives  42.2 us (8%)
  between operations  14.9 us (3%)
  local copies, waits for them, and re-layouts  13.7 us (2%)
    reduce_scatter x2, waiting for transfers between devices, per_device(): lax.psum_scatter(mat_grad, ('wide', 'narrow'), scatter_dimension=0, tiled...  184 us
    all_gather x2, waiting for transfers between devices, per_device(): lax.all_gather(matrices[layer_index], ('wide', 'narrow'), axis=0, tiled=T...  104 us
    psum x1, blocking collectives, per_device(): vec_total = lax.psum(jnp.stack(vec_list), ('wide', 'narrow'))  42.2 us
    convert_element_type x2, other arithmetic, backward_layer(): pull_gelu(jnp.concatenate([grad_gate, grad_value], axis=1))[0]  22.9 us
    dot_general x2, matrix products, forward_parts(): jnp.einsum('td,fd->tf', normed, w_in_t, preferred_element_type=jnp.float32)  19.6 us
    concatenate x2, other arithmetic, backward_layer(): mat_grad = jnp.concatenate([grad_w_in_t, grad_w_out, grad_spatial], axis=0)  19.1 us
    dot_general x2, matrix products, backward_layer(): jnp.einsum('td,cd->tc', grad_branch, w_out, preferred_element_type=jnp.fl...  15 us
    dot_general x2, matrix products, backward_layer(): jnp.einsum('tf,fd->td', grad_pre, w_in_t, preferred_element_type=jnp.floa...  14.2 us
  transfers between devices with their start and end apart: 4, of which 4 were waited for; matrix products, arithmetic and copies ran while one was open for 19% of the time, Pallas kernels for 0%

commit v1 on v0

v1 whole, which is shorter than its diff:
```python
import functools

import jax
import jax.numpy as jnp
from jax import lax
from jax.experimental import pallas as pl
from jax.experimental.pallas import tpu as pltpu
from jax.sharding import PartitionSpec as P

D = 512
FF = 3072
HALF = FF // 2
S = 512
LAYERS = 2
VEC = D + HALF + S
ALL_ROWS = FF + HALF + S
EPSILON = 1e-05
BLOCK = 512
MESH = pl.DeviceIdType.MESH
BF16 = jnp.bfloat16
F32 = jnp.float32
GELU_A = 0.7978845608028654
GELU_B = 0.044715


def dot(left, right, left_dim, right_dim):
    dims = (((left_dim,), (right_dim,)), ((), ()))
    return lax.dot_general(left, right, dims, preferred_element_type=F32)


def gelu_and_slope(z):
    squared = z * z
    tanh = jnp.tanh(z * (GELU_A + (GELU_A * GELU_B) * squared))
    half_z = 0.5 * z
    value = half_z + half_z * tanh
    slope = (0.5 + 0.5 * tanh) + (half_z * (1.0 - tanh * tanh)) * (
        GELU_A + (3.0 * GELU_A * GELU_B) * squared
    )
    return value, slope


def lane_groups(values):
    total = values[:, :128]
    for at in range(128, values.shape[1], 128):
        total = total + values[:, at : at + 128]
    return total


def lanes(column, width):
    return jnp.concatenate([column] * (width // 128), axis=1)


class Links:
    def __init__(self, wide, narrow, share):
        self.share = share
        self.levels = wide // 2
        self.narrow = narrow
        self.w = lax.axis_index("wide")
        self.n = lax.axis_index("narrow")
        self.x = self.w % 2
        self.z = self.w // 2
        self.core = self.n % 2
        self.y = self.n // 2
        other_w = self.w + 1 - 2 * self.x
        other_n = self.n + 2 - 4 * self.y
        self.first = self.mix((other_w, self.n), (self.w, other_n))
        self.second = self.mix((self.w, other_n), (other_w, self.n))
        self.twin = (self.w, self.n + 1 - 2 * self.core)
        self.along_x = (other_w, self.n)
        self.along_y = (self.w, other_n)

    def mix(self, zero, one):
        return tuple((1 - self.core) * a + self.core * b for a, b in zip(zero, one))

    def line(self, z):
        return (2 * z + self.x, self.n)

    def partners(self):
        found = [self.twin, self.first, self.second]
        for step in range(1, self.levels):
            found.append(self.line((self.z + step) % self.levels))
        return found

    def rows(self, w, n):
        return pl.ds(pl.multiple_of((w * self.narrow + n) * self.share, 16), self.share)

    def shards(self, z):
        out = []
        for n, n_first, n_second, w_first, w_second in (
            (self.n, self.first[1], self.second[1], self.first[0], self.second[0]),
            (
                self.twin[1],
                self.twin[1] + (1 - self.core) * (2 - 4 * self.y),
                self.twin[1] + self.core * (2 - 4 * self.y),
                self.w + self.core * (1 - 2 * self.x),
                self.w + (1 - self.core) * (1 - 2 * self.x),
            ),
        ):
            cross = n + 2 - 4 * self.y
            out.append(self.rows(2 * z + self.x, n))
            out.append(self.rows(2 * z + w_first % 2, n_first))
            out.append(self.rows(2 * z + w_second % 2, n_second))
            out.append(self.rows(2 * z + 1 - self.x, cross))
        return out


def send(source, target, send_sem, recv_sem, device):
    return pltpu.make_async_remote_copy(
        src_ref=source,
        dst_ref=target,
        send_sem=send_sem,
        recv_sem=recv_sem,
        device_id=device,
        device_id_type=MESH,
    )


def kernel(wide, narrow, linked, tok, seg, mats, vec, cot, *refs):
    out, grad_in, mat_out, vec_out, park_u, park_s, park_n, park_g = refs[:8]
    (
        weights,
        grads,
        landing,
        u,
        gp,
        s,
        n,
        tmp,
        a,
        xf,
        xb,
        masked,
        masked_t,
        rstd_in,
        rstd_mid,
        acc1,
        acc2,
        seg_t,
        bias_t,
        bias_sum,
        gains,
        inv_gains,
        vec_sum,
        vec_in,
        local_sem,
        credit,
        g_send,
        g_recv,
        r_send,
        r_recv,
        v_send,
        v_recv,
    ) = refs[8:]
    tokens = xf.shape[0]
    rows_here = tokens // S
    share = mats.shape[1]
    links = Links(wide, narrow, share) if linked else None
    levels = wide // 2
    passed_on, started = ([], []), []

    load_tok = pltpu.make_async_copy(tok, xb, local_sem.at[0])
    load_tok.start()
    load_mats = []
    for layer in range(LAYERS):
        place = links.rows(links.w, links.n) if linked else pl.ds(0, ALL_ROWS)
        copy = pltpu.make_async_copy(
            mats.at[layer], weights.at[layer, place], local_sem.at[1 + layer]
        )
        copy.start()
        load_mats.append(copy)

    if linked:
        barrier = pltpu.get_barrier_semaphore()
        for device in links.partners():
            pl.semaphore_signal(barrier, inc=1, device_id=device, device_id_type=MESH)
        pl.semaphore_wait(barrier, len(links.partners()))

    def pass_on(layer, z, slot, rows, target_slot, send_slot, device):
        copy = send(
            weights.at[layer, rows],
            weights.at[layer, rows],
            g_send.at[layer, z, send_slot],
            g_recv.at[layer, z, target_slot],
            device,
        )
        copy.start()
        passed_on[layer].append(copy)

    def arrived(layer, z, slot, rows):
        send(
            weights.at[layer, rows],
            weights.at[layer, rows],
            g_send.at[layer, z, 0],
            g_recv.at[layer, z, slot],
            links.twin,
        ).wait_recv()

    def gather_own(layer):
        load_mats[layer].wait()
        shards = links.shards(links.z)
        for step in range(1, levels):
            copy = send(
                weights.at[layer, shards[0]],
                weights.at[layer, shards[0]],
                g_send.at[layer, step, 7],
                g_recv.at[layer, links.z, 0],
                links.line((links.z + step) % levels),
            )
            copy.start()
            passed_on[layer].append(copy)
        gather_from_line(layer, 0)

    def gather_from_line(layer, step):
        z = (links.z + step) % levels
        shards = links.shards(z)
        if step:
            arrived(layer, z, 0, shards[0])
        pass_on(layer, z, 0, shards[0], 1, 0, links.first)
        pass_on(layer, z, 0, shards[0], 2, 1, links.second)
        pass_on(layer, z, 0, shards[0], 4, 3, links.twin)

    def gather_from_first(layer, step):
        z = (links.z + step) % levels
        shards = links.shards(z)
        arrived(layer, z, 1, shards[1])
        pass_on(layer, z, 1, shards[1], 3, 2, links.second)
        pass_on(layer, z, 1, shards[1], 5, 4, links.twin)

    def gather_from_second(layer, step):
        z = (links.z + step) % levels
        shards = links.shards(z)
        for slot in (2, 3):
            arrived(layer, z, slot, shards[slot])
            pass_on(layer, z, slot, shards[slot], 4 + slot, 3 + slot, links.twin)

    def gather_from_twin(layer, step):
        z = (links.z + step) % levels
        shards = links.shards(z)
        for slot in range(4, 8):
            arrived(layer, z, slot, shards[slot])

    def gather_all(layer, parts):
        for part in parts:
            for step in range(levels):
                if part is not gather_from_line or step:
                    part(layer, step)

    def land(layer, index):
        rows = pl.ds(pl.multiple_of(index * share, 16), share)
        return weights.at[1, rows] if layer == 0 else landing.at[rows]

    def add_in(layer, rows, index):
        grads[layer, rows, :] = (
            grads[layer, rows, :].astype(F32) + land(layer, index)[...].astype(F32)
        ).astype(BF16)

    def reduce_copy(layer, z, rows, target, slot, device, recv_z=None):
        return send(
            grads.at[layer, rows],
            land(layer, target),
            r_send.at[layer, z, slot],
            r_recv.at[layer, z if recv_z is None else recv_z, slot],
            device,
        )

    def reduce_begin(layer, z):
        shards = links.shards(z)
        for slot in range(4):
            copy = reduce_copy(layer, z, shards[4 + slot], 4 * z + slot, slot, links.twin)
            copy.start()
            started.append(copy)

    def reduce_second(layer, z):
        shards = links.shards(z)
        for slot in (2, 3, 0, 1):
            reduce_copy(layer, z, shards[slot], 4 * z + slot, slot, links.twin).wait_recv()
            add_in(layer, shards[slot], 4 * z + slot)
            if slot >= 2:
                copy = reduce_copy(
                    layer, z, shards[slot], 4 * levels + 2 * z + slot - 2, 2 + slot, links.second
                )
                copy.start()
                started.append(copy)

    def reduce_first(layer, z):
        shards = links.shards(z)
        for slot in (1, 0):
            index = 4 * levels + 2 * z + slot
            reduce_copy(layer, z, shards[slot], index, 4 + slot, links.second).wait_recv()
            add_in(layer, shards[slot], index)
            if slot == 1:
                copy = reduce_copy(layer, z, shards[1], 6 * levels + z, 6, links.first)
                copy.start()
                started.append(copy)

    def line_copy(layer, z):
        return reduce_copy(
            layer, z, links.shards(z)[0], 7 * levels + links.z, 7, links.line(z), links.z
        )

    def reduce_line(layer, z):
        shards = links.shards(z)
        index = 6 * levels + z
        reduce_copy(layer, z, shards[0], index, 6, links.first).wait_recv()
        add_in(layer, shards[0], index)

        @pl.when(links.z != z)
        def _():
            line_copy(layer, z).start()

    def reduce_end(layer):
        shards = links.shards(links.z)
        total = grads[layer, shards[0], :].astype(F32)
        for step in range(1, levels):
            z = (links.z + step) % levels
            reduce_copy(layer, z, shards[0], 7 * levels + z, 7, links.line(z)).wait_recv()
            total = total + land(layer, 7 * levels + z)[...].astype(F32)
        mat_out[layer] = total
        for z in range(levels):

            @pl.when(links.z != z)
            def _():
                line_copy(layer, z).wait_send()

    gains[...] = vec[...].astype(F32)
    inv_gains[...] = 1.0 / gains[...]
    for r in range(rows_here):
        line = jnp.broadcast_to(seg[r : r + 1, :].astype(F32), (128, S))
        seg_t[r] = line.T

    def same(r):
        return lanes(seg_t[r], S) == seg[r : r + 1, :].astype(F32)

    def row_chunk(i, size):
        return pl.ds(pl.multiple_of(i * size, size), size)

    def norm_in(layer):
        gain = gains[layer : layer + 1, :D]

        @pl.loop(0, tokens // 128)
        def _(i):
            rows = row_chunk(i, 128)
            values = xb[rows, :].astype(F32) if layer == 0 else xf[rows, :]
            center = values - jnp.mean(values, axis=1, keepdims=True)
            scale = lax.rsqrt(jnp.mean(center * center, axis=1, keepdims=True) + EPSILON)
            a[layer, rows, :] = (center * scale * gain).astype(BF16)
            rstd_in[layer, rows, :] = jnp.broadcast_to(scale, (128, 128))

    def hidden_gate(layer):
        @pl.loop(0, HALF // BLOCK)
        def _(i):
            cols = row_chunk(i, BLOCK)
            for r in range(rows_here):
                rows = pl.ds(r * S, S)
                z = dot(a[layer, rows, :], weights[layer, cols, :], 1, 1)
                value, slope = gelu_and_slope(z)
                u[rows, cols] = value.astype(BF16)
                gp[rows, cols] = slope.astype(BF16)

    def hidden_value(layer):
        acc1[...] = jnp.zeros_like(acc1)

        @pl.loop(0, HALF // BLOCK)
        def _(i):
            cols = row_chunk(i, BLOCK)
            cols_all = pl.ds(pl.multiple_of(HALF + i * BLOCK, BLOCK), BLOCK)
            for r in range(rows_here):
                rows = pl.ds(r * S, S)
                z = dot(a[layer, rows, :], weights[layer, cols_all, :], 1, 1)
                value, slope = gelu_and_slope(z)
                n[rows, cols] = value.astype(BF16)
                gp[rows, cols_all] = slope.astype(BF16)
                acc1[rows, :] += lane_groups(value)

    def norm_mid(layer):
        gain = gains[layer : layer + 1, D : D + HALF]

        @pl.loop(0, tokens // 64)
        def _(i):
            rows = row_chunk(i, 64)
            mean = jnp.sum(acc1[rows, :], axis=1, keepdims=True) * (1.0 / HALF)
            center = n[rows, :].astype(F32) - mean
            scale = lax.rsqrt(jnp.mean(center * center, axis=1, keepdims=True) + EPSILON)
            n[rows, :] = (center * scale * gain).astype(BF16)
            rstd_mid[layer, rows, :] = jnp.broadcast_to(scale, (64, 128))

    def mask_weights(layer):
        spatial = weights[layer, FF + HALF :, :].astype(F32)
        spatial_t = spatial.T
        for r in range(rows_here):
            keep = same(r)
            masked[r] = jnp.where(keep, spatial, 0.0).astype(BF16)
            masked_t[r] = jnp.where(keep, spatial_t, 0.0).astype(BF16)
        line = jnp.broadcast_to(gains[layer : layer + 1, D + HALF :], (128, S))
        bias_t[...] = line.T

    def mix(layer):
        @pl.loop(0, HALF // BLOCK)
        def _(i):
            cols = row_chunk(i, BLOCK)
            for r in range(rows_here):
                rows = pl.ds(r * S, S)
                mixed = dot(masked[r], n[rows, cols], 1, 0) + lanes(bias_t[...], BLOCK)
                s[rows, cols] = mixed.astype(BF16)
                tmp[rows, cols] = (u[rows, cols].astype(F32) * mixed).astype(BF16)

    def project(layer):
        @pl.loop(0, tokens // S)
        def _(i):
            rows = row_chunk(i, S)
            values = xb[rows, :].astype(F32) if layer == 0 else xf[rows, :]
            xf[rows, :] = values + dot(tmp[rows, :], weights[layer, FF : FF + HALF, :], 1, 0)

    def back_project(layer):
        bias_sum[...] = jnp.zeros_like(bias_sum)

        @pl.loop(0, HALF // BLOCK)
        def _(i):
            cols = row_chunk(i, BLOCK)
            w_rows = pl.ds(pl.multiple_of(FF + i * BLOCK, BLOCK), BLOCK)
            for r in range(rows_here):
                rows = pl.ds(r * S, S)
                dy = dot(xb[rows, :], weights[layer, w_rows, :], 1, 1)
                gate = u[rows, cols].astype(F32)
                mixed = s[rows, cols].astype(F32)
                ds = (dy * gate).astype(BF16)
                u[rows, cols] = (gate * mixed).astype(BF16)
                s[rows, cols] = ds
                gp[rows, cols] = (dy * mixed * gp[rows, cols].astype(F32)).astype(BF16)
                bias_sum[...] += lane_groups(ds.astype(F32))
            grads[layer, w_rows, :] = dot(u[:, cols], xb[...], 0, 0).astype(BF16)

    def back_input_weights(layer, low, high):
        @pl.loop(low, high)
        def _(i):
            cols = row_chunk(i, BLOCK)
            grads[layer, cols, :] = dot(gp[:, cols], a[layer], 0, 0).astype(BF16)

    def back_spatial(layer):
        total = None
        for r in range(rows_here):
            rows = pl.ds(r * S, S)
            outer = jnp.where(same(r), dot(s[rows, :], n[rows, :], 1, 1), 0.0)
            total = outer if total is None else total + outer
        grads[layer, FF + HALF :, :] = total.astype(BF16)
        at = layer * VEC + D + HALF
        vec_sum[:, at : at + S] = jnp.sum(bias_sum[...].T, axis=0, keepdims=True)

    def back_mix(layer):
        acc1[...] = jnp.zeros_like(acc1)
        acc2[...] = jnp.zeros_like(acc2)

        @pl.loop(0, HALF // BLOCK)
        def _(i):
            cols = row_chunk(i, BLOCK)
            at = pl.ds(pl.multiple_of(D + i * BLOCK, BLOCK), BLOCK)
            to = pl.ds(pl.multiple_of(layer * VEC + D + i * BLOCK, BLOCK), BLOCK)
            column = jnp.zeros((1, BLOCK), F32)
            for r in range(rows_here):
                rows = pl.ds(r * S, S)
                dn = dot(masked_t[r], s[rows, cols], 1, 0)
                e = dn * gains[layer : layer + 1, at]
                dn_n = dn * n[rows, cols].astype(F32)
                tmp[rows, cols] = e.astype(BF16)
                acc1[rows, :] += lane_groups(e)
                acc2[rows, :] += lane_groups(dn_n)
                column = column + jnp.sum(dn_n, axis=0, keepdims=True)
            vec_sum[:, to] = column * inv_gains[layer : layer + 1, at]

    def back_norm_mid(layer):
        inverse = inv_gains[layer : layer + 1, D : D + HALF]

        @pl.loop(0, tokens // 64)
        def _(i):
            rows = row_chunk(i, 64)
            mean_e = jnp.sum(acc1[rows, :], axis=1, keepdims=True) * (1.0 / HALF)
            mean_ew = jnp.sum(acc2[rows, :], axis=1, keepdims=True) * (1.0 / HALF)
            w = n[rows, :].astype(F32) * inverse
            dv = tmp[rows, :].astype(F32) - mean_e - w * mean_ew
            dv = dv * lanes(rstd_mid[layer, rows, :], HALF)
            gp[rows, HALF:] = (dv * gp[rows, HALF:].astype(F32)).astype(BF16)

    def back_input(layer):
        gain = gains[layer : layer + 1, :D]
        inverse = inv_gains[layer : layer + 1, :D]
        at = layer * VEC
        vec_sum[:, at : at + D] = jnp.zeros((1, D), F32)

        @pl.loop(0, tokens // S)
        def _(i):
            rows = row_chunk(i, S)
            da = dot(gp[rows, :], weights[layer, :FF, :], 1, 0)
            normed = a[layer, rows, :].astype(F32)
            product = da * normed
            e = da * gain
            mean_e = jnp.mean(e, axis=1, keepdims=True)
            mean_ew = jnp.mean(product, axis=1, keepdims=True)
            dx = (e - mean_e - normed * inverse * mean_ew) * lanes(rstd_in[layer, rows, :], D)
            upper = xb[rows, :].astype(F32) if layer == LAYERS - 1 else xf[rows, :]
            total = upper + dx
            xf[rows, :] = total
            if layer:
                xb[rows, :] = total.astype(BF16)
            vec_sum[:, at : at + D] += jnp.sum(product, axis=0, keepdims=True) * inverse

    parts = (gather_from_line, gather_from_first, gather_from_second, gather_from_twin)
    if linked:
        gather_own(0)
    load_tok.wait()
    norm_in(0)
    if linked:
        gather_all(0, parts[:1])
        gather_own(1)
        gather_all(0, parts[1:])
    else:
        load_mats[0].wait()
    hidden_gate(0)
    keep_u = pltpu.make_async_copy(u, park_u, local_sem.at[3])
    keep_u.start()
    if linked:
        gather_all(1, parts[:1])
    hidden_value(0)
    keep_g = pltpu.make_async_copy(gp, park_g, local_sem.at[4])
    keep_g.start()
    if linked:
        gather_all(1, parts[1:2])
    mask_weights(0)
    norm_mid(0)
    keep_n = pltpu.make_async_copy(n, park_n, local_sem.at[5])
    keep_n.start()
    mix(0)
    keep_s = pltpu.make_async_copy(s, park_s, local_sem.at[6])
    keep_s.start()
    if linked:
        gather_all(1, parts[2:3])
    project(0)
    load_cot = pltpu.make_async_copy(cot, xb, local_sem.at[0])
    load_cot.start()
    norm_in(1)
    if linked:
        gather_all(1, parts[3:])
    else:
        load_mats[1].wait()
    keep_u.wait()
    keep_g.wait()
    hidden_gate(1)
    keep_n.wait()
    hidden_value(1)
    mask_weights(1)
    norm_mid(1)
    keep_s.wait()
    mix(1)
    project(1)
    write_out = pltpu.make_async_copy(xf, out, local_sem.at[1])
    write_out.start()
    load_cot.wait()

    back_project(1)
    back_input_weights(1, 0, HALF // BLOCK)
    load_u = pltpu.make_async_copy(park_u, u, local_sem.at[3])
    load_u.start()
    if linked:
        reduce_begin(1, 0)
    back_spatial(1)
    if linked:
        reduce_begin(1, levels - 1)
        reduce_second(1, 0)
    back_mix(1)
    load_s = pltpu.make_async_copy(park_s, s, local_sem.at[6])
    load_s.start()
    if linked:
        reduce_second(1, levels - 1)
    back_norm_mid(1)
    load_n = pltpu.make_async_copy(park_n, n, local_sem.at[5])
    load_n.start()
    if linked:
        reduce_first(1, 0)
    back_input_weights(1, HALF // BLOCK, FF // BLOCK)
    if linked:
        for z in range(levels - 2, 0, -1):
            reduce_begin(1, z)
        reduce_first(1, levels - 1)
        reduce_line(1, 0)
    write_out.wait()
    back_input(1)
    load_g = pltpu.make_async_copy(park_g, gp, local_sem.at[4])
    load_g.start()
    if linked:
        for copy in passed_on[1]:
            copy.wait_send()
        for device in links.partners():
            pl.semaphore_signal(credit, inc=1, device_id=device, device_id_type=MESH)
        reduce_line(1, levels - 1)
        for z in range(levels - 2, 0, -1):
            reduce_second(1, z)

    mask_weights(0)
    load_u.wait()
    load_s.wait()
    load_g.wait()
    back_project(0)
    if linked:
        for z in range(levels - 2, 0, -1):
            reduce_first(1, z)
    back_input_weights(0, 0, HALF // BLOCK)
    if linked:
        pl.semaphore_wait(credit, len(links.partners()))
        reduce_begin(0, 0)
        for z in range(levels - 2, 0, -1):
            reduce_line(1, z)
    load_n.wait()
    back_spatial(0)
    if linked:
        reduce_begin(0, levels - 1)
        reduce_second(0, 0)
        reduce_end(1)
    back_mix(0)
    if linked:
        reduce_second(0, levels - 1)
        reduce_first(0, 0)
    back_norm_mid(0)
    back_input_weights(0, HALF // BLOCK, FF // BLOCK)
    if linked:
        for z in range(levels - 2, 0, -1):
            reduce_begin(0, z)
        reduce_first(0, levels - 1)
        reduce_line(0, 0)
        for z in range(levels - 2, 0, -1):
            reduce_second(0, z)
        reduce_line(0, levels - 1)
    back_input(0)
    write_in = pltpu.make_async_copy(xf, grad_in, local_sem.at[0])
    write_in.start()
    if linked:
        for z in range(levels - 2, 0, -1):
            reduce_first(0, z)
        for index, device in ((0, links.twin), (1, links.along_y), (2, links.along_x)):
            copy = send(
                vec_sum, vec_in.at[levels + index], v_send.at[index], v_recv.at[index], device
            )
            copy.start()
            copy.wait()
            vec_sum[...] = vec_sum[...] + vec_in[levels + index]
        copies = []
        for step in range(1, levels):
            z = (links.z + step) % levels
            copy = send(
                vec_sum, vec_in.at[links.z], v_send.at[2 + step], v_recv.at[3 + links.z], links.line(z)
            )
            copy.start()
            copies.append(copy)
        for z in range(levels - 2, 0, -1):
            reduce_line(0, z)
        for step in range(1, levels):
            z = (links.z + step) % levels
            send(
                vec_sum, vec_in.at[z], v_send.at[2 + step], v_recv.at[3 + z], links.line(z)
            ).wait_recv()
        for copy in copies:
            copy.wait_send()
        vec_in[pl.ds(links.z, 1)] = vec_sum[...][None]
        total = vec_in[0]
        for z in range(1, levels):
            total = total + vec_in[z]
        reduce_end(0)
        for copy in passed_on[0] + started:
            copy.wait_send()
    else:
        total = vec_sum[...]
        for layer in range(LAYERS):
            copy = pltpu.make_async_copy(grads.at[layer], mat_out.at[layer], local_sem.at[1])
            copy.start()
            copy.wait()
    for layer in range(LAYERS):
        vec_out[layer : layer + 1, :] = total[:, layer * VEC : (layer + 1) * VEC]
    write_in.wait()


def per_device(wide, narrow, tokens, segment_ids, matrices, vectors, cotangent):
    axes = ("wide", "narrow")
    count, share = tokens.shape[0], matrices.shape[1]
    total = count * S
    linked = narrow == 4 and wide % 2 == 0 and wide >= 8 and share % 16 == 0
    if not linked:
        matrices = lax.all_gather(matrices, axes, axis=1, tiled=True)
    levels = wide // 2
    anywhere = pl.BlockSpec(memory_space=pl.ANY)
    vmem = pl.BlockSpec(memory_space=pltpu.VMEM)
    mat_shape = (LAYERS, share, D) if linked else (LAYERS, ALL_ROWS, D)
    half, full = (total, HALF), (total, FF)
    dma = pltpu.SemaphoreType.DMA
    flags = dict(collective_id=0) if linked else {}
    results = pl.pallas_call(
        functools.partial(kernel, wide, narrow, linked),
        out_shape=(
            jax.ShapeDtypeStruct((total, D), F32),
            jax.ShapeDtypeStruct((total, D), F32),
            jax.ShapeDtypeStruct(mat_shape, F32 if linked else BF16),
            jax.ShapeDtypeStruct((LAYERS, VEC), F32),
            jax.ShapeDtypeStruct(half, BF16),
            jax.ShapeDtypeStruct(half, BF16),
            jax.ShapeDtypeStruct(half, BF16),
            jax.ShapeDtypeStruct(full, BF16),
        ),
        in_specs=[anywhere, vmem, anywhere, vmem, anywhere],
        out_specs=(anywhere, anywhere, vmem if linked else anywhere, vmem) + (anywhere,) * 4,
        scratch_shapes=[
            pltpu.VMEM((LAYERS, ALL_ROWS, D), BF16),
            pltpu.VMEM((LAYERS, ALL_ROWS, D), BF16),
            pltpu.VMEM((ALL_ROWS if linked else 16, D), BF16),
            pltpu.VMEM(half, BF16),
            pltpu.VMEM(full, BF16),
            pltpu.VMEM(half, BF16),
            pltpu.VMEM(half, BF16),
            pltpu.VMEM(half, BF16),
            pltpu.VMEM((LAYERS, total, D), BF16),
            pltpu.VMEM((total, D), F32),
            pltpu.VMEM((total, D), BF16),
            pltpu.VMEM((count, S, S), BF16),
            pltpu.VMEM((count, S, S), BF16),
            pltpu.VMEM((LAYERS, total, 128), F32),
            pltpu.VMEM((LAYERS, total, 128), F32),
            pltpu.VMEM((total, 128), F32),
            pltpu.VMEM((total, 128), F32),
            pltpu.VMEM((count, S, 128), F32),
            pltpu.VMEM((S, 128), F32),
            pltpu.VMEM((S, 128), F32),
            pltpu.VMEM((LAYERS, VEC), F32),
            pltpu.VMEM((LAYERS, VEC), F32),
            pltpu.VMEM((1, LAYERS * VEC), F32),
            pltpu.VMEM((levels + 3, 1, LAYERS * VEC), F32),
            dma((7,)),
            pltpu.SemaphoreType.REGULAR,
            dma((LAYERS, levels, 8)),
            dma((LAYERS, levels, 8)),
            dma((LAYERS, levels, 8)),
            dma((LAYERS, levels, 8)),
            dma((levels + 3,)),
            dma((levels + 3,)),
        ],
        compiler_params=pltpu.CompilerParams(
            has_side_effects=True, vmem_limit_bytes=63 << 20, **flags
        ),
    )(
        tokens.reshape(total, D),
        segment_ids,
        matrices,
        vectors,
        cotangent.reshape(total, D),
    )
    out, grad_in, mat_grads, vec_grads = results[:4]
    if not linked:
        mat_grads = lax.psum_scatter(
            mat_grads.astype(F32), axes, scatter_dimension=1, tiled=True
        )
        vec_grads = lax.psum(vec_grads, axes)
    return (out.reshape(tokens.shape), grad_in.reshape(tokens.shape), mat_grads, vec_grads)


def solution(mesh):
    rows = P(("wide", "narrow"), None, None)
    spread = P(None, ("wide", "narrow"), None)
    return jax.shard_map(
        functools.partial(per_device, mesh.shape["wide"], mesh.shape["narrow"]),
        mesh=mesh,
        in_specs=(rows, P(("wide", "narrow"), None), spread, P(), rows),
        out_specs=(rows, rows, spread, P()),
        check_vma=False,
    )
```

time: 553 us -> 181 us (0.33)
  the two profiles are of different devices: /device:TPU:0 before, /device:TPU:8 now
where the time goes in v1:
time: 181 us
  Pallas kernels  174 us (96%)
  local copies, waits for them, and re-layouts  6.21 us (3%)
    pallas_call x1, Pallas kernels, per_device(): pl.pallas_call(functools.partial(kernel, wide, narrow, linked), out_shape...  174 us
    unnamed x10, local copies, waits for them, and re-layouts  6.21 us

profile of v1, /device:TPU:8, one launch (start us, length us, event | category | flops | bytes accessed | tf_op | source)
XLA Modules:
  0.0 180.6 jit_solution(5125325327865184089)
XLA Ops:
  0.6 173.8 %shard_map.84 = (f32[1024,512]{1,0:T(8,128)}, f32[1024,512]{1,0:T(8,128)}, f32[2,160,512]{2,1,0:T(8,128)}, f32[2,2560]{1,0:T(2,128)}, bf16[1024,1536]{1,0:T(8,12...) custom-call(bf16[1024,512]{1,0:T(8,128)(2,1)} %bitcast.6, ...), custom_call_target="tpu_custom_call" | custom-call | tf_op jit(solution)/shard_map/pallas_call | solution.py:693
  174.4 0.0 copy-start
  174.4 3.2 %copy.13 = f32[2,512,512]{2,1,0:T(8,128)} copy(f32[2,512,512]{2,1,0:T(8,128)} %bitcast.5) | data formatting | bytes 4194304
  177.7 0.0 copy-done
  177.7 0.0 copy-start.1
  177.7 0.0 copy-start.2
  177.7 1.3 copy.14
  179.0 0.2 copy-done.1
  179.2 0.8 copy.15
  180.0 0.0 copy-done.2
  180.0 0.6 copy.16
Async XLA Ops:
  174.4 3.2 %copy-start = (f32[1024,512]{1,0:T(8,128)S(1)}, f32[1024,512]{1,0:T(8,128)}, u32[]{:S(2)}) copy-start(f32[1024,512]{1,0:T(8,128)} %get-tuple-element.9) | copy-start | bytes 6291460
  177.7 1.5 copy-start.1
  177.7 2.4 %copy-start.2 = (f32[2,2560]{1,0:T(2,128)S(1)}, f32[2,2560]{1,0:T(2,128)}, u32[]{:S(2)}) copy-start(f32[2,2560]{1,0:T(2,128)} %get-tuple-element.19) | copy-start | bytes 61444

commit v2 on v1

v2 whole, which is shorter than its diff:
```python
import functools

import jax
import jax.numpy as jnp
from jax import lax
from jax.experimental import pallas as pl
from jax.experimental.pallas import tpu as pltpu
from jax.sharding import PartitionSpec as P

D = 512
FF = 3072
HALF = FF // 2
S = 512
LAYERS = 2
VEC = D + HALF + S
ALL_ROWS = FF + HALF + S
EPSILON = 1e-05
BLOCK = 512
PART = 256
WIDTH = 256
MESH = pl.DeviceIdType.MESH
BF16 = jnp.bfloat16
F32 = jnp.float32
GELU_A = 0.7978845608028654
GELU_B = 0.044715


def dot(left, right, left_dim, right_dim):
    dims = (((left_dim,), (right_dim,)), ((), ()))
    return lax.dot_general(left, right, dims, preferred_element_type=F32)


def gelu_and_slope(z):
    squared = z * z
    share = 0.5 + 0.5 * jnp.tanh(z * (GELU_A + (GELU_A * GELU_B) * squared))
    value = z * share
    near, gate = value.astype(BF16), share.astype(BF16)
    rise = BF16(2.0 * GELU_A) + BF16(6.0 * GELU_A * GELU_B) * squared.astype(BF16)
    return value, gate + (near - near * gate) * rise


def lane_groups(values):
    total = values[:, :128]
    for at in range(128, values.shape[1], 128):
        total = total + values[:, at : at + 128]
    return total


def lanes(column, width):
    return jnp.concatenate([column] * (width // 128), axis=1)


class Links:
    def __init__(self, wide, narrow, share):
        self.share = share
        self.levels = wide // 2
        self.narrow = narrow
        self.w = lax.axis_index("wide")
        self.n = lax.axis_index("narrow")
        self.x = self.w % 2
        self.z = self.w // 2
        self.core = self.n % 2
        self.y = self.n // 2
        other_w = self.w + 1 - 2 * self.x
        other_n = self.n + 2 - 4 * self.y
        self.first = self.mix((other_w, self.n), (self.w, other_n))
        self.second = self.mix((self.w, other_n), (other_w, self.n))
        self.twin = (self.w, self.n + 1 - 2 * self.core)
        self.along_x = (other_w, self.n)
        self.along_y = (self.w, other_n)

    def mix(self, zero, one):
        return tuple((1 - self.core) * a + self.core * b for a, b in zip(zero, one))

    def line(self, z):
        return (2 * z + self.x, self.n)

    def partners(self):
        found = [self.twin, self.first, self.second]
        for step in range(1, self.levels):
            found.append(self.line((self.z + step) % self.levels))
        return found

    def rows(self, w, n):
        return pl.ds(pl.multiple_of((w * self.narrow + n) * self.share, 16), self.share)

    def shards(self, z):
        out = []
        for n, n_first, n_second, w_first, w_second in (
            (self.n, self.first[1], self.second[1], self.first[0], self.second[0]),
            (
                self.twin[1],
                self.twin[1] + (1 - self.core) * (2 - 4 * self.y),
                self.twin[1] + self.core * (2 - 4 * self.y),
                self.w + self.core * (1 - 2 * self.x),
                self.w + (1 - self.core) * (1 - 2 * self.x),
            ),
        ):
            cross = n + 2 - 4 * self.y
            out.append(self.rows(2 * z + self.x, n))
            out.append(self.rows(2 * z + w_first % 2, n_first))
            out.append(self.rows(2 * z + w_second % 2, n_second))
            out.append(self.rows(2 * z + 1 - self.x, cross))
        return out


def send(source, target, send_sem, recv_sem, device):
    return pltpu.make_async_remote_copy(
        src_ref=source,
        dst_ref=target,
        send_sem=send_sem,
        recv_sem=recv_sem,
        device_id=device,
        device_id_type=MESH,
    )


def kernel(wide, narrow, linked, tok, seg, mats, vec, cot, *refs):
    out, grad_in, mat_out, vec_out, park_u, park_s, park_n, park_g = refs[:8]
    (
        weights,
        grads,
        landing,
        u,
        gp,
        s,
        n,
        a,
        xf,
        xb,
        masked,
        masked_t,
        rstd_in,
        rstd_mid,
        acc1,
        acc2,
        vf,
        mat_stage,
        seg_t,
        bias_t,
        bias_sum,
        gains,
        inv_gains,
        vec_sum,
        vec_in,
        local_sem,
        credit,
        g_send,
        g_recv,
        r_send,
        r_recv,
        v_send,
        v_recv,
    ) = refs[8:]
    tokens = xf.shape[0]
    rows_here = tokens // S
    share = mats.shape[1]
    links = Links(wide, narrow, share) if linked else None
    levels = wide // 2 if linked else 4
    passed_on, started = ([], []), []

    load_tok = pltpu.make_async_copy(tok, xb, local_sem.at[0])
    load_tok.start()
    load_mats = []
    for layer in range(LAYERS):
        place = links.rows(links.w, links.n) if linked else pl.ds(0, ALL_ROWS)
        copy = pltpu.make_async_copy(
            mats.at[layer], weights.at[layer, place], local_sem.at[1 + layer]
        )
        copy.start()
        load_mats.append(copy)

    if linked:
        barrier = pltpu.get_barrier_semaphore()
        for device in links.partners():
            pl.semaphore_signal(barrier, inc=1, device_id=device, device_id_type=MESH)
        pl.semaphore_wait(barrier, len(links.partners()))

    if linked:
        sources, targets = [], []
        for step in range(levels):
            below = (links.z - step + 2 * levels) // (2 * levels)
            sources.append(below * (links.z - step) + (1 - below) * step)
        for step in range(1, levels):
            above = (levels - 1 - links.z - step + 2 * levels) // (2 * levels)
            upward = links.z + step
            downward = levels - 1 - step
            targets.append(links.line(above * upward + (1 - above) * downward))
        not_top = links.z < levels - 1
        shards_of = [links.shards(z) for z in sources]

    def gather_copy(layer, step, slot, send_slot, target_slot, device):
        rows = shards_of[step][slot]
        return send(
            weights.at[layer, rows],
            weights.at[layer, rows],
            g_send.at[layer, sources[step], send_slot],
            g_recv.at[layer, sources[step], target_slot],
            device,
        )

    def pass_on(layer, step, slot, send_slot, target_slot, device):
        again = functools.partial(gather_copy, layer, step, slot, send_slot, target_slot, device)
        again().start()
        passed_on[layer].append(again)

    def arrived(layer, step, slot):
        gather_copy(layer, step, slot, 0, slot, links.twin).wait_recv()

    def gather_depart(layer):
        load_mats[layer].wait()
        for at, device in enumerate(targets):
            pass_on(layer, 0, 0, 7 + at, 0, device)

    def gather_line(layer, step):
        if step:
            arrived(layer, step, 0)
        pass_on(layer, step, 0, 0, 1, links.first)
        pass_on(layer, step, 0, 1, 2, links.second)
        pass_on(layer, step, 0, 3, 4, links.twin)

    def gather_first(layer, step):
        arrived(layer, step, 1)
        pass_on(layer, step, 1, 2, 3, links.second)
        pass_on(layer, step, 1, 4, 5, links.twin)

    def gather_second(layer, step):
        for slot in (2, 3):
            arrived(layer, step, slot)
            pass_on(layer, step, slot, 3 + slot, 4 + slot, links.twin)

    def gather_twin(layer, step):
        for slot in range(4, 8):
            arrived(layer, step, slot)

    def gather_sent(layer):
        for again in passed_on[layer]:
            again().wait_send()

    if linked:
        shards_at = [links.shards(z) for z in range(levels)]
        own_shards = links.shards(links.z)

    def land(layer, index):
        rows = pl.ds(pl.multiple_of(index * share, 16), share)
        return weights.at[1, rows] if layer == 0 else landing.at[rows]

    def add_in(layer, rows, index):
        grads[layer, rows, :] = (
            grads[layer, rows, :].astype(F32) + land(layer, index)[...].astype(F32)
        ).astype(BF16)

    def reduce_copy(layer, z, rows, target, slot, device, recv_z=None):
        return send(
            grads.at[layer, rows],
            land(layer, target),
            r_send.at[layer, z, slot],
            r_recv.at[layer, z if recv_z is None else recv_z, slot],
            device,
        )

    def reduce_start(*where):
        reduce_copy(*where).start()
        started.append(where)

    def reduce_begin(layer, z):
        shards = shards_at[z]
        for slot in range(4):
            reduce_start(layer, z, shards[4 + slot], 4 * z + slot, slot, links.twin)

    def reduce_second(layer, z):
        shards = shards_at[z]
        for slot in (2, 3, 0, 1):
            reduce_copy(layer, z, shards[slot], 4 * z + slot, slot, links.twin).wait_recv()
            add_in(layer, shards[slot], 4 * z + slot)
            if slot >= 2:
                index = 4 * levels + 2 * z + slot - 2
                reduce_start(layer, z, shards[slot], index, 2 + slot, links.second)

    def reduce_first(layer, z):
        shards = shards_at[z]
        for slot in (1, 0):
            index = 4 * levels + 2 * z + slot
            reduce_copy(layer, z, shards[slot], index, 4 + slot, links.second).wait_recv()
            add_in(layer, shards[slot], index)
            if slot == 1:
                reduce_start(layer, z, shards[1], 6 * levels + z, 6, links.first)

    def line_copy(layer, z):
        return reduce_copy(
            layer, z, shards_at[z][0], 7 * levels + links.z, 7, links.line(z), links.z
        )

    def reduce_line(layer, z):
        shards = shards_at[z]
        index = 6 * levels + z
        reduce_copy(layer, z, shards[0], index, 6, links.first).wait_recv()
        add_in(layer, shards[0], index)

        @pl.when(links.z != z)
        def _():
            line_copy(layer, z).start()

    def mat_copy(layer):
        return pltpu.make_async_copy(mat_stage.at[layer], mat_out.at[layer], local_sem.at[1 + layer])

    def reduce_end(layer):
        shards = own_shards
        total = grads[layer, shards[0], :].astype(F32)
        for step in range(1, levels):
            z = (links.z + step) % levels
            reduce_copy(layer, z, shards[0], 7 * levels + z, 7, links.line(z)).wait_recv()
            total = total + land(layer, 7 * levels + z)[...].astype(F32)
        mat_stage[layer] = total
        mat_copy(layer).start()
        for z in range(levels):

            @pl.when(links.z != z)
            def _():
                line_copy(layer, z).wait_send()

    def vec_pair(index, device):
        return send(vec_sum, vec_in.at[levels + index], v_send.at[index], v_recv.at[index], device)

    def vec_add(index, device):
        vec_pair(index, device).wait()
        vec_sum[...] = vec_sum[...] + vec_in[levels + index]

    def vec_copy(step, z):
        return send(
            vec_sum,
            vec_in.at[z],
            v_send.at[2 + step],
            v_recv.at[3 + z],
            links.line((links.z + step) % levels),
        )

    def vec_line_begin():
        for step in range(1, levels):
            vec_copy(step, links.z).start()

    def vec_line_end():
        for step in range(1, levels):
            vec_copy(step, (links.z + step) % levels).wait_recv()
        for step in range(1, levels):
            vec_copy(step, links.z).wait_send()
        vec_in[pl.ds(links.z, 1)] = vec_sum[...][None]
        total = vec_in[0]
        for z in range(1, levels):
            total = total + vec_in[z]
        return total

    def prepare():
        gains[...] = vec[...].astype(F32)
        inv_gains[...] = 1.0 / gains[...]
        for r in range(rows_here):
            line = jnp.broadcast_to(seg[r : r + 1, :].astype(F32), (128, S))
            seg_t[r] = line.T
        acc1[...] = jnp.zeros_like(acc1)

    def same(r):
        return lanes(seg_t[r], S) == seg[r : r + 1, :].astype(F32)

    def row_chunk(i, size):
        return pl.ds(pl.multiple_of(i * size, size), size)

    def between(i, hooks):
        for at, hook in enumerate(hooks):
            if hook is not None:
                pl.when(i == at)(hook)

    def norm_in(layer):
        gain = gains[layer : layer + 1, :D]

        @pl.loop(0, tokens // 256)
        def _(i):
            found = []
            for part in range(2):
                rows = row_chunk(2 * i + part, 128)
                values = xb[rows, :].astype(F32) if layer == 0 else xf[rows, :]
                mean = jnp.sum(lane_groups(values), axis=1, keepdims=True) * (1.0 / D)
                found.append((rows, values - mean))
            for at, (rows, center) in enumerate(found):
                spread = jnp.sum(lane_groups(center * center), axis=1, keepdims=True) * (1.0 / D)
                found[at] = (rows, center, lax.rsqrt(spread + EPSILON))
            for rows, center, scale in found:
                a[layer, rows, :] = (center * scale * gain).astype(BF16)
                rstd_in[layer, rows, :] = jnp.broadcast_to(scale, (128, 128))

    def hidden(layer, z):
        per_level = ALL_ROWS // levels // WIDTH
        low, high, half = z * per_level, (z + 1) * per_level, HALF // WIDTH

        @pl.loop(jnp.minimum(low, half), jnp.minimum(high, half))
        def _(i):
            cols = row_chunk(i, WIDTH)
            for at in range(0, tokens, PART):
                rows = pl.ds(at, PART)
                value, slope = gelu_and_slope(dot(a[layer, rows, :], weights[layer, cols, :], 1, 1))
                u[rows, cols] = value.astype(BF16)
                gp[rows, cols] = slope

        @pl.loop(jnp.clip(low, half, 2 * half), jnp.clip(high, half, 2 * half))
        def _(i):
            cols_all = row_chunk(i, WIDTH)
            cols = row_chunk(i - half, WIDTH)
            for at in range(0, tokens, PART):
                rows = pl.ds(at, PART)
                z = dot(a[layer, rows, :], weights[layer, cols_all, :], 1, 1)
                value, slope = gelu_and_slope(z)
                vf[rows, cols] = value
                gp[rows, cols_all] = slope
                acc1[rows, :] += lane_groups(value)

    def norm_mid(layer):
        gain = gains[layer : layer + 1, D : D + HALF]
        for r in range(rows_here):
            rows = pl.ds(r * S, S)
            mean = jnp.sum(acc1[rows, :], axis=1, keepdims=True) * (1.0 / HALF)
            acc1[rows, :] = jnp.broadcast_to(mean, (S, 128))

        @pl.loop(0, tokens // 64)
        def _(i):
            rows = row_chunk(i, 64)
            center = vf[rows, :] - lanes(acc1[rows, :], HALF)
            acc2[rows, :] = lane_groups(center * center)

        for r in range(rows_here):
            rows = pl.ds(r * S, S)
            spread = jnp.sum(acc2[rows, :], axis=1, keepdims=True) * (1.0 / HALF)
            rstd_mid[layer, rows, :] = jnp.broadcast_to(lax.rsqrt(spread + EPSILON), (S, 128))

        @pl.loop(0, tokens // 64)
        def _(i):
            rows = row_chunk(i, 64)
            center = vf[rows, :] - lanes(acc1[rows, :], HALF)
            n[rows, :] = (center * lanes(rstd_mid[layer, rows, :], HALF) * gain).astype(BF16)

    def mask_weights(layer):
        spatial = weights[layer, FF + HALF :, :].astype(F32)
        spatial_t = spatial.T
        for r in range(rows_here):
            keep = same(r)
            masked[r] = jnp.where(keep, spatial, 0.0).astype(BF16)
            masked_t[r] = jnp.where(keep, spatial_t, 0.0).astype(BF16)
        line = jnp.broadcast_to(gains[layer : layer + 1, D + HALF :], (128, S))
        bias_t[...] = line.T

    def gated_rows(block, at, size):
        return pl.ds(pl.multiple_of(block * tokens + at, PART), size)

    def mix(layer, hooks=()):
        @pl.loop(0, HALF // BLOCK)
        def _(i):
            between(i, hooks)
            cols = row_chunk(i, BLOCK)
            for r in range(rows_here):
                for at in range(0, S, PART):
                    rows = pl.ds(r * S + at, PART)
                    mixed = dot(masked[r, at : at + PART, :], n[r * S : r * S + S, cols], 1, 0)
                    mixed = mixed + lanes(bias_t[at : at + PART, :], BLOCK)
                    s[rows, cols] = mixed.astype(BF16)
                    gated = (u[rows, cols].astype(F32) * mixed).astype(BF16)
                    grads[0, gated_rows(i, r * S + at, PART), :] = gated

    def project(layer, hooks=()):
        @pl.loop(0, tokens // S)
        def _(i):
            between(i, hooks)
            rows = row_chunk(i, S)
            values = xb[rows, :].astype(F32) if layer == 0 else xf[rows, :]
            for k in range(HALF // BLOCK):
                part = weights[layer, FF + k * BLOCK : FF + (k + 1) * BLOCK, :]
                values = values + dot(grads[0, gated_rows(k, i * S, S), :], part, 1, 0)
            xf[rows, :] = values

    def back_project(layer, hooks=()):
        @pl.loop(0, HALF // BLOCK)
        def _(i):
            between(i, hooks)
            cols = row_chunk(i, BLOCK)
            w_rows = pl.ds(pl.multiple_of(FF + i * BLOCK, BLOCK), BLOCK)
            for at in range(0, tokens, PART):
                rows, here = pl.ds(at, PART), pl.ds(at % S, PART)
                dy = dot(xb[rows, :], weights[layer, w_rows, :], 1, 1).astype(BF16)
                gate, mixed = u[rows, cols], s[rows, cols]
                ds = dy * gate
                u[rows, cols] = gate * mixed
                s[rows, cols] = ds
                gp[rows, cols] = dy * mixed * gp[rows, cols]
                part = lane_groups(ds.astype(F32))
                if at < S:
                    part = part + jnp.where(i == 0, 0.0, bias_sum[here, :])
                else:
                    part = part + bias_sum[here, :]
                bias_sum[here, :] = part
            grads[layer, w_rows, :] = dot(u[:, cols], xb[...], 0, 0).astype(BF16)

    def back_input_weights(layer, low, hooks=(), turn=0):
        count = HALF // BLOCK

        @pl.loop(0, count)
        def _(i):
            between(i, hooks)
            cols = row_chunk(low + lax.rem(i + turn, count), BLOCK)
            grads[layer, cols, :] = dot(gp[:, cols], a[layer], 0, 0).astype(BF16)

    def back_spatial(layer):
        total = None
        for r in range(rows_here):
            rows = pl.ds(r * S, S)
            outer = jnp.where(same(r), dot(s[rows, :], n[rows, :], 1, 1), 0.0)
            total = outer if total is None else total + outer
        grads[layer, FF + HALF :, :] = total.astype(BF16)
        at = layer * VEC + D + HALF
        vec_sum[:, at : at + S] = jnp.sum(bias_sum[...].T, axis=0, keepdims=True)

    def back_mix(layer, hooks=()):
        @pl.loop(0, HALF // BLOCK)
        def _(i):
            between(i, hooks)
            cols = row_chunk(i, BLOCK)
            at_cols = pl.ds(pl.multiple_of(D + i * BLOCK, BLOCK), BLOCK)
            to = pl.ds(pl.multiple_of(layer * VEC + D + i * BLOCK, BLOCK), BLOCK)
            column = jnp.zeros((8, BLOCK), F32)
            for r in range(rows_here):
                for at in range(0, S, PART):
                    rows = pl.ds(r * S + at, PART)
                    dn = dot(masked_t[r, at : at + PART, :], s[r * S : r * S + S, cols], 1, 0)
                    e = dn * gains[layer : layer + 1, at_cols]
                    dn_n = dn * n[rows, cols].astype(F32)
                    vf[rows, cols] = e
                    part_e, part_ew = lane_groups(e), lane_groups(dn_n)
                    acc1[rows, :] = jnp.where(i == 0, part_e, acc1[rows, :] + part_e)
                    acc2[rows, :] = jnp.where(i == 0, part_ew, acc2[rows, :] + part_ew)
                    column = column + jnp.sum(dn_n.reshape(PART // 8, 8, BLOCK), axis=0)
            column = jnp.sum(column, axis=0, keepdims=True)
            vec_sum[:, to] = column * inv_gains[layer : layer + 1, at_cols]

    def back_norm_mid(layer):
        inverse = inv_gains[layer : layer + 1, D : D + HALF]
        for r in range(rows_here):
            rows = pl.ds(r * S, S)
            for acc in (acc1, acc2):
                mean = jnp.sum(acc[rows, :], axis=1, keepdims=True) * (1.0 / HALF)
                acc[rows, :] = jnp.broadcast_to(mean, (S, 128))

        @pl.loop(0, tokens // 64)
        def _(i):
            rows = row_chunk(i, 64)
            mean_e = lanes(acc1[rows, :], HALF)
            mean_ew = lanes(acc2[rows, :], HALF)
            dv = vf[rows, :] - mean_e - n[rows, :].astype(F32) * inverse * mean_ew
            dv = (dv * lanes(rstd_mid[layer, rows, :], HALF)).astype(BF16)
            gp[rows, HALF:] = dv * gp[rows, HALF:]

    def back_input(layer, hooks=()):
        gain = gains[layer : layer + 1, :D]
        inverse = inv_gains[layer : layer + 1, :D]
        at = layer * VEC
        vec_sum[:, at : at + D] = jnp.zeros((1, D), F32)

        @pl.loop(0, tokens // PART)
        def _(i):
            between(i, hooks)
            rows = row_chunk(i, PART)
            da = dot(gp[rows, :], weights[layer, :FF, :], 1, 0)
            normed = a[layer, rows, :].astype(F32)
            product = da * normed
            e = da * gain
            mean_e = jnp.sum(lane_groups(e), axis=1, keepdims=True) * (1.0 / D)
            mean_ew = jnp.sum(lane_groups(product), axis=1, keepdims=True) * (1.0 / D)
            dx = (e - mean_e - normed * inverse * mean_ew) * lanes(rstd_in[layer, rows, :], D)
            above = xb[rows, :].astype(F32) if layer == LAYERS - 1 else xf[rows, :]
            total = above + dx
            xf[rows, :] = total
            if layer:
                xb[rows, :] = total.astype(BF16)
            vec_sum[:, at : at + D] += jnp.sum(product, axis=0, keepdims=True) * inverse

    def later(act, *where):
        return (lambda: act(*where)) if linked else None

    def norm_mid_early(layer, early):
        if linked:
            pl.when(not_top if early else jnp.logical_not(not_top))(lambda: norm_mid(layer))
        elif not early:
            norm_mid(layer)

    def take(layer, step):
        if linked:
            gather_twin(layer, step)
        hidden(layer, sources[step] if linked else step)

    if linked:
        gather_depart(0)
        gather_line(0, 0)
        prepare()
        load_tok.wait()
        norm_in(0)
        gather_line(0, 1)
        gather_first(0, 0)
        gather_line(0, 2)
        gather_first(0, 1)
        gather_second(0, 0)
        take(0, 0)
        gather_first(0, 2)
        gather_second(0, 1)
        gather_line(0, 3)
        gather_depart(1)
        take(0, 1)
        gather_second(0, 2)
        gather_first(0, 3)
        gather_line(1, 0)
        take(0, 2)
        gather_second(0, 3)
        gather_line(1, 1)
        gather_first(1, 0)
    else:
        prepare()
        for copy in load_mats:
            copy.wait()
        load_tok.wait()
        norm_in(0)
        for step in range(levels - 1):
            take(0, step)
    norm_mid_early(0, True)
    take(0, levels - 1)
    norm_mid_early(0, False)
    keep_u = pltpu.make_async_copy(u, park_u, local_sem.at[3])
    keep_u.start()
    keep_g = pltpu.make_async_copy(gp, park_g, local_sem.at[4])
    keep_g.start()
    keep_n = pltpu.make_async_copy(n, park_n, local_sem.at[5])
    keep_n.start()
    mask_weights(0)
    mix(0, (later(gather_line, 1, 2), later(gather_first, 1, 1), None))
    keep_s = pltpu.make_async_copy(s, park_s, local_sem.at[6])
    keep_s.start()
    project(0, (None, later(gather_second, 1, 0)))
    load_cot = pltpu.make_async_copy(cot, xb, local_sem.at[0])
    load_cot.start()
    norm_in(1)
    acc1[...] = jnp.zeros_like(acc1)
    keep_u.wait()
    keep_g.wait()
    for step in range(levels - 1):
        take(1, step)
        if linked:
            if step < 2:
                gather_first(1, step + 2)
            gather_second(1, step + 1)
            if step == 0:
                gather_line(1, 3)
    keep_n.wait()
    norm_mid_early(1, True)
    take(1, levels - 1)
    norm_mid_early(1, False)
    mask_weights(1)
    keep_s.wait()
    mix(1)
    load_cot.wait()

    back_project(1)
    back_input_weights(1, 0)
    load_u = pltpu.make_async_copy(park_u, u, local_sem.at[3])
    load_u.start()
    if linked:
        reduce_begin(1, 0)
    project(1)
    write_out = pltpu.make_async_copy(xf, out, local_sem.at[1])
    write_out.start()
    if linked:
        reduce_second(1, 0)
    back_spatial(1)
    if linked:
        reduce_begin(1, 3)
    back_mix(1, (None, later(reduce_second, 1, 3), None))
    load_s = pltpu.make_async_copy(park_s, s, local_sem.at[6])
    load_s.start()
    back_norm_mid(1)
    load_n = pltpu.make_async_copy(park_n, n, local_sem.at[5])
    load_n.start()
    if linked:
        reduce_first(1, 0)
    half = HALF // BLOCK
    back_input_weights(1, half, (None, later(reduce_begin, 1, 2), later(reduce_second, 1, 2)), 2)
    if linked:
        reduce_begin(1, 1)
        reduce_first(1, 3)
    write_out.wait()
    back_input(1, (later(reduce_second, 1, 1), None, later(reduce_line, 1, 0), None))
    load_g = pltpu.make_async_copy(park_g, gp, local_sem.at[4])
    load_g.start()
    if linked:
        gather_sent(1)
        for device in links.partners():
            pl.semaphore_signal(credit, inc=1, device_id=device, device_id_type=MESH)
        reduce_first(1, 2)

    mask_weights(0)
    load_u.wait()
    load_s.wait()
    load_g.wait()
    back_project(0, (None, later(reduce_line, 1, 3), None))
    back_input_weights(0, 0, (later(reduce_first, 1, 1), None, later(reduce_line, 1, 2)))
    if linked:
        pl.semaphore_wait(credit, len(links.partners()))
        reduce_begin(0, 0)
    load_n.wait()
    back_spatial(0)
    if linked:
        reduce_second(0, 0)
        reduce_begin(0, 3)
    back_mix(0, (None, later(reduce_second, 0, 3), later(reduce_line, 1, 1)))
    back_norm_mid(0)
    if linked:
        reduce_first(0, 0)
    back_input_weights(0, half, (None, later(reduce_begin, 0, 2), later(reduce_second, 0, 2)), 2)
    if linked:
        reduce_begin(0, 1)
        reduce_first(0, 3)
        reduce_end(1)
    back_input(0, (later(reduce_second, 0, 1), None, later(reduce_line, 0, 0), None))
    write_in = pltpu.make_async_copy(xf, grad_in, local_sem.at[0])
    write_in.start()
    if linked:
        vec_pair(0, links.twin).start()
        reduce_first(0, 2)
        vec_add(0, links.twin)
        vec_pair(1, links.along_y).start()
        reduce_line(0, 3)
        vec_add(1, links.along_y)
        vec_pair(2, links.along_x).start()
        reduce_first(0, 1)
        vec_add(2, links.along_x)
        vec_line_begin()
        reduce_line(0, 2)
        reduce_line(0, 1)
        total = vec_line_end()
        reduce_end(0)
        gather_sent(0)
        for where in started:
            reduce_copy(*where).wait_send()
        for layer in range(LAYERS):
            mat_copy(layer).wait()
    else:
        total = vec_sum[...]
        for layer in range(LAYERS):
            copy = pltpu.make_async_copy(grads.at[layer], mat_out.at[layer], local_sem.at[1])
            copy.start()
            copy.wait()
    for layer in range(LAYERS):
        vec_out[layer : layer + 1, :] = total[:, layer * VEC : (layer + 1) * VEC]
    write_in.wait()


def per_device(wide, narrow, tokens, segment_ids, matrices, vectors, cotangent):
    axes = ("wide", "narrow")
    count, share = tokens.shape[0], matrices.shape[1]
    total = count * S
    linked = narrow == 4 and wide == 8 and share % 16 == 0
    if not linked:
        matrices = lax.all_gather(matrices, axes, axis=1, tiled=True)
    levels = wide // 2 if linked else 4
    anywhere = pl.BlockSpec(memory_space=pl.ANY)
    vmem = pl.BlockSpec(memory_space=pltpu.VMEM)
    mat_shape = (LAYERS, share, D) if linked else (LAYERS, ALL_ROWS, D)
    half, full = (total, HALF), (total, FF)
    dma = pltpu.SemaphoreType.DMA
    flags = dict(collective_id=0) if linked else {}
    results = pl.pallas_call(
        functools.partial(kernel, wide, narrow, linked),
        out_shape=(
            jax.ShapeDtypeStruct((total, D), F32),
            jax.ShapeDtypeStruct((total, D), F32),
            jax.ShapeDtypeStruct(mat_shape, F32 if linked else BF16),
            jax.ShapeDtypeStruct((LAYERS, VEC), F32),
            jax.ShapeDtypeStruct(half, BF16),
            jax.ShapeDtypeStruct(half, BF16),
            jax.ShapeDtypeStruct(half, BF16),
            jax.ShapeDtypeStruct(full, BF16),
        ),
        in_specs=[anywhere, vmem, anywhere, vmem, anywhere],
        out_specs=(anywhere, anywhere, anywhere, vmem) + (anywhere,) * 4,
        scratch_shapes=[
            pltpu.VMEM((LAYERS, ALL_ROWS, D), BF16),
            pltpu.VMEM((LAYERS, ALL_ROWS, D), BF16),
            pltpu.VMEM((ALL_ROWS if linked else 16, D), BF16),
            pltpu.VMEM(half, BF16),
            pltpu.VMEM(full, BF16),
            pltpu.VMEM(half, BF16),
            pltpu.VMEM(half, BF16),
            pltpu.VMEM((LAYERS, total, D), BF16),
            pltpu.VMEM((total, D), F32),
            pltpu.VMEM((total, D), BF16),
            pltpu.VMEM((count, S, S), BF16),
            pltpu.VMEM((count, S, S), BF16),
            pltpu.VMEM((LAYERS, total, 128), F32),
            pltpu.VMEM((LAYERS, total, 128), F32),
            pltpu.VMEM((total, 128), F32),
            pltpu.VMEM((total, 128), F32),
            pltpu.VMEM((total, HALF), F32),
            pltpu.VMEM((LAYERS, share if linked else 8, D), F32),
            pltpu.VMEM((count, S, 128), F32),
            pltpu.VMEM((S, 128), F32),
            pltpu.VMEM((S, 128), F32),
            pltpu.VMEM((LAYERS, VEC), F32),
            pltpu.VMEM((LAYERS, VEC), F32),
            pltpu.VMEM((1, LAYERS * VEC), F32),
            pltpu.VMEM((levels + 3, 1, LAYERS * VEC), F32),
            dma((7,)),
            pltpu.SemaphoreType.REGULAR,
            dma((LAYERS, levels, 7 + levels)),
            dma((LAYERS, levels, 8)),
            dma((LAYERS, levels, 8)),
            dma((LAYERS, levels, 8)),
            dma((levels + 3,)),
            dma((levels + 3,)),
        ],
        compiler_params=pltpu.CompilerParams(
            has_side_effects=True, vmem_limit_bytes=63 << 20, **flags
        ),
    )(
        tokens.reshape(total, D),
        segment_ids,
        matrices,
        vectors,
        cotangent.reshape(total, D),
    )
    out, grad_in, mat_grads, vec_grads = results[:4]
    if not linked:
        mat_grads = lax.psum_scatter(
            mat_grads.astype(F32), axes, scatter_dimension=1, tiled=True
        )
        vec_grads = lax.psum(vec_grads, axes)
    return (out.reshape(tokens.shape), grad_in.reshape(tokens.shape), mat_grads, vec_grads)


def solution(mesh):
    rows = P(("wide", "narrow"), None, None)
    spread = P(None, ("wide", "narrow"), None)
    return jax.shard_map(
        functools.partial(per_device, mesh.shape["wide"], mesh.shape["narrow"]),
        mesh=mesh,
        in_specs=(rows, P(("wide", "narrow"), None), spread, P(), rows),
        out_specs=(rows, rows, spread, P()),
        check_vma=False,
    )
```

time: 181 us -> 156 us (0.86)
  Pallas kernels: 174 us -> 149 us
    pallas_call x1, Pallas kernels: 174 us -> 149 us  [per_device(): pl.pallas_call(functools.partial(kernel, wide, narrow, linked), out_shape...]
where the time goes in v2:
time: 156 us
  Pallas kernels  149 us (96%)
  local copies, waits for them, and re-layouts  6.21 us (4%)
    pallas_call x1, Pallas kernels, per_device(): pl.pallas_call(functools.partial(kernel, wide, narrow, linked), out_shape...  149 us
    unnamed x10, local copies, waits for them, and re-layouts  6.21 us

profile of v2, /device:TPU:8, one launch (start us, length us, event | category | flops | bytes accessed | tf_op | source)
XLA Modules:
  0.0 155.7 jit_solution(10031652796916076171)
XLA Ops:
  0.6 148.8 %shard_map.84 = (f32[1024,512]{1,0:T(8,128)}, f32[1024,512]{1,0:T(8,128)}, f32[2,160,512]{2,1,0:T(8,128)}, f32[2,2560]{1,0:T(2,128)}, bf16[1024,1536]{1,0:T(8,12...) custom-call(bf16[1024,512]{1,0:T(8,128)(2,1)} %bitcast.6, ...), custom_call_target="tpu_custom_call" | custom-call | tf_op jit(solution)/shard_map/pallas_call | solution.py:772
  149.4 0.0 copy-start
  149.5 3.2 %copy.13 = f32[2,512,512]{2,1,0:T(8,128)} copy(f32[2,512,512]{2,1,0:T(8,128)} %bitcast.5) | data formatting | bytes 4194304
  152.7 0.0 copy-done
  152.7 0.0 copy-start.1
  152.7 0.0 copy-start.2
  152.7 1.3 copy.14
  154.0 0.2 copy-done.1
  154.2 0.8 copy.15
  155.1 0.0 copy-done.2
  155.1 0.6 copy.16
Async XLA Ops:
  149.4 3.2 %copy-start = (f32[1024,512]{1,0:T(8,128)S(1)}, f32[1024,512]{1,0:T(8,128)}, u32[]{:S(2)}) copy-start(f32[1024,512]{1,0:T(8,128)} %get-tuple-element.9) | copy-start | bytes 6291460
  152.7 1.5 copy-start.1
  152.7 2.4 %copy-start.2 = (f32[2,2560]{1,0:T(2,128)S(1)}, f32[2,2560]{1,0:T(2,128)}, u32[]{:S(2)}) copy-start(f32[2,2560]{1,0:T(2,128)} %get-tuple-element.19) | copy-start | bytes 61444

commit v3 on v2

--- a/solution.py
+++ b/solution.py
@@ -263,6 +263,11 @@
         reduce_copy(*where).start()
         started.append(where)
 
+    def reduce_sent(layer):
+        for where in started:
+            if where[0] == layer:
+                reduce_copy(*where).wait_send()
+
     def reduce_begin(layer, z):
         shards = shards_at[z]
         for slot in range(4):
@@ -474,7 +479,7 @@
                 values = values + dot(grads[0, gated_rows(k, i * S, S), :], part, 1, 0)
             xf[rows, :] = values
 
-    def back_project(layer, hooks=()):
+    def back_project(layer, hooks=(), weights_too=True):
         @pl.loop(0, HALF // BLOCK)
         def _(i):
             between(i, hooks)
@@ -494,7 +499,14 @@
                 else:
                     part = part + bias_sum[here, :]
                 bias_sum[here, :] = part
-            grads[layer, w_rows, :] = dot(u[:, cols], xb[...], 0, 0).astype(BF16)
+            if weights_too:
+                grads[layer, w_rows, :] = dot(u[:, cols], xb[...], 0, 0).astype(BF16)
+
+    def back_output_weights(layer):
+        @pl.loop(0, HALF // BLOCK)
+        def _(i):
+            w_rows = pl.ds(pl.multiple_of(FF + i * BLOCK, BLOCK), BLOCK)
+            grads[layer, w_rows, :] = dot(u[:, row_chunk(i, BLOCK)], xb[...], 0, 0).astype(BF16)
 
     def back_input_weights(layer, low, hooks=(), turn=0):
         count = HALF // BLOCK
@@ -581,16 +593,19 @@
     def later(act, *where):
         return (lambda: act(*where)) if linked else None
 
-    def norm_mid_early(layer, early):
-        if linked:
-            pl.when(not_top if early else jnp.logical_not(not_top))(lambda: norm_mid(layer))
-        elif not early:
-            norm_mid(layer)
-
-    def take(layer, step):
-        if linked:
-            gather_twin(layer, step)
-        hidden(layer, sources[step] if linked else step)
+    def levels_in_turn(layer, after):
+        last = levels - 2 + links.z // (levels - 1) if linked else levels - 1
+
+        @pl.loop(0, levels)
+        def _(step):
+            if linked:
+                between(step, [functools.partial(gather_twin, layer, k) for k in range(levels)])
+                below = (links.z - step + 2 * levels) // (2 * levels)
+                hidden(layer, below * (links.z - step) + (1 - below) * step)
+                between(step, after)
+            else:
+                hidden(layer, step)
+            pl.when(step == last)(lambda: norm_mid(layer))
 
     if linked:
         gather_depart(0)
@@ -603,30 +618,30 @@
         gather_line(0, 2)
         gather_first(0, 1)
         gather_second(0, 0)
-        take(0, 0)
-        gather_first(0, 2)
-        gather_second(0, 1)
-        gather_line(0, 3)
-        gather_depart(1)
-        take(0, 1)
-        gather_second(0, 2)
-        gather_first(0, 3)
-        gather_line(1, 0)
-        take(0, 2)
-        gather_second(0, 3)
-        gather_line(1, 1)
-        gather_first(1, 0)
     else:
         prepare()
         for copy in load_mats:
             copy.wait()
         load_tok.wait()
         norm_in(0)
-        for step in range(levels - 1):
-            take(0, step)
-    norm_mid_early(0, True)
-    take(0, levels - 1)
-    norm_mid_early(0, False)
+
+    def after_first():
+        gather_first(0, 2)
+        gather_second(0, 1)
+        gather_line(0, 3)
+        gather_depart(1)
+
+    def after_second():
+        gather_second(0, 2)
+        gather_first(0, 3)
+        gather_line(1, 0)
+
+    def after_third():
+        gather_second(0, 3)
+        gather_line(1, 1)
+        gather_first(1, 0)
+
+    levels_in_turn(0, (after_first, after_second, after_third))
     keep_u = pltpu.make_async_copy(u, park_u, local_sem.at[3])
     keep_u.start()
     keep_g = pltpu.make_async_copy(gp, park_g, local_sem.at[4])
@@ -644,38 +659,46 @@
     acc1[...] = jnp.zeros_like(acc1)
     keep_u.wait()
     keep_g.wait()
-    for step in range(levels - 1):
-        take(1, step)
-        if linked:
-            if step < 2:
-                gather_first(1, step + 2)
-            gather_second(1, step + 1)
-            if step == 0:
-                gather_line(1, 3)
     keep_n.wait()
-    norm_mid_early(1, True)
-    take(1, levels - 1)
-    norm_mid_early(1, False)
+
+    def after_first_again():
+        gather_first(1, 2)
+        gather_second(1, 1)
+        gather_line(1, 3)
+
+    def after_second_again():
+        gather_first(1, 3)
+        gather_second(1, 2)
+
+    def after_third_again():
+        gather_second(1, 3)
+
+    if linked:
+        gather_sent(0)
+    levels_in_turn(1, (after_first_again, after_second_again, after_third_again))
     mask_weights(1)
     keep_s.wait()
     mix(1)
     load_cot.wait()
 
-    back_project(1)
+    back_project(1, weights_too=False)
     back_input_weights(1, 0)
+    if linked:
+        reduce_begin(1, 0)
+    back_output_weights(1)
     load_u = pltpu.make_async_copy(park_u, u, local_sem.at[3])
     load_u.start()
     if linked:
-        reduce_begin(1, 0)
+        reduce_second(1, 0)
+    back_spatial(1)
+    if linked:
+        reduce_begin(1, 3)
     project(1)
     write_out = pltpu.make_async_copy(xf, out, local_sem.at[1])
     write_out.start()
     if linked:
-        reduce_second(1, 0)
-    back_spatial(1)
-    if linked:
-        reduce_begin(1, 3)
-    back_mix(1, (None, later(reduce_second, 1, 3), None))
+        reduce_second(1, 3)
+    back_mix(1)
     load_s = pltpu.make_async_copy(park_s, s, local_sem.at[6])
     load_s.start()
     back_norm_mid(1)
@@ -721,27 +744,26 @@
         reduce_begin(0, 1)
         reduce_first(0, 3)
         reduce_end(1)
+        reduce_sent(1)
     back_input(0, (later(reduce_second, 0, 1), None, later(reduce_line, 0, 0), None))
     write_in = pltpu.make_async_copy(xf, grad_in, local_sem.at[0])
     write_in.start()
     if linked:
         vec_pair(0, links.twin).start()
         reduce_first(0, 2)
+        reduce_first(0, 1)
         vec_add(0, links.twin)
         vec_pair(1, links.along_y).start()
         reduce_line(0, 3)
         vec_add(1, links.along_y)
         vec_pair(2, links.along_x).start()
-        reduce_first(0, 1)
+        reduce_line(0, 2)
         vec_add(2, links.along_x)
         vec_line_begin()
-        reduce_line(0, 2)
         reduce_line(0, 1)
+        reduce_sent(0)
+        reduce_end(0)
         total = vec_line_end()
-        reduce_end(0)
-        gather_sent(0)
-        for where in started:
-            reduce_copy(*where).wait_send()
         for layer in range(LAYERS):
             mat_copy(layer).wait()
     else:

time: 156 us -> 156 us (level)
  no operation moved by 1% of the time
where the time goes in v3:
time: 156 us; the launch traced here: 155 us
  Pallas kernels  148 us (95%)
  local copies, waits for them, and re-layouts  6.21 us (4%)
    pallas_call x1, Pallas kernels, per_device(): pl.pallas_call(functools.partial(kernel, wide, narrow, linked), out_shape...  148 us
    unnamed x10, local copies, waits for them, and re-layouts  6.21 us

profile of v3, /device:TPU:8, one launch (start us, length us, event | category | flops | bytes accessed | tf_op | source)
XLA Modules:
  0.0 155.3 jit_solution(10156576029346882585)
XLA Ops:
  0.6 148.4 %shard_map.84 = (f32[1024,512]{1,0:T(8,128)}, f32[1024,512]{1,0:T(8,128)}, f32[2,160,512]{2,1,0:T(8,128)}, f32[2,2560]{1,0:T(2,128)}, bf16[1024,1536]{1,0:T(8,12...) custom-call(bf16[1024,512]{1,0:T(8,128)(2,1)} %bitcast.6, ...), custom_call_target="tpu_custom_call" | custom-call | tf_op jit(solution)/shard_map/pallas_call | solution.py:794
  149.0 0.0 copy-start
  149.0 3.2 %copy.13 = f32[2,512,512]{2,1,0:T(8,128)} copy(f32[2,512,512]{2,1,0:T(8,128)} %bitcast.5) | data formatting | bytes 4194304
  152.3 0.0 copy-done
  152.3 0.0 copy-start.1
  152.3 0.0 copy-start.2
  152.3 1.3 copy.14
  153.6 0.2 copy-done.1
  153.8 0.8 copy.15
  154.6 0.0 copy-done.2
  154.6 0.6 copy.16
Async XLA Ops:
  149.0 3.2 %copy-start = (f32[1024,512]{1,0:T(8,128)S(1)}, f32[1024,512]{1,0:T(8,128)}, u32[]{:S(2)}) copy-start(f32[1024,512]{1,0:T(8,128)} %get-tuple-element.9) | copy-start | bytes 6291460
  152.3 1.5 copy-start.1
  152.3 2.4 %copy-start.2 = (f32[2,2560]{1,0:T(2,128)S(1)}, f32[2,2560]{1,0:T(2,128)}, u32[]{:S(2)}) copy-start(f32[2,2560]{1,0:T(2,128)} %get-tuple-element.19) | copy-start | bytes 61444

commit v4 on v3

--- a/solution.py
+++ b/solution.py
@@ -399,8 +399,8 @@
         @pl.loop(jnp.minimum(low, half), jnp.minimum(high, half))
         def _(i):
             cols = row_chunk(i, WIDTH)
-            for at in range(0, tokens, PART):
-                rows = pl.ds(at, PART)
+            for at in range(0, tokens, S):
+                rows = pl.ds(at, S)
                 value, slope = gelu_and_slope(dot(a[layer, rows, :], weights[layer, cols, :], 1, 1))
                 u[rows, cols] = value.astype(BF16)
                 gp[rows, cols] = slope
@@ -409,8 +409,8 @@
         def _(i):
             cols_all = row_chunk(i, WIDTH)
             cols = row_chunk(i - half, WIDTH)
-            for at in range(0, tokens, PART):
-                rows = pl.ds(at, PART)
+            for at in range(0, tokens, S):
+                rows = pl.ds(at, S)
                 z = dot(a[layer, rows, :], weights[layer, cols_all, :], 1, 1)
                 value, slope = gelu_and_slope(z)
                 vf[rows, cols] = value
@@ -477,7 +477,10 @@
             for k in range(HALF // BLOCK):
                 part = weights[layer, FF + k * BLOCK : FF + (k + 1) * BLOCK, :]
                 values = values + dot(grads[0, gated_rows(k, i * S, S), :], part, 1, 0)
-            xf[rows, :] = values
+            if layer == LAYERS - 1:
+                masked[i] = values.astype(BF16)
+            else:
+                xf[rows, :] = values
 
     def back_project(layer, hooks=(), weights_too=True):
         @pl.loop(0, HALF // BLOCK)
@@ -585,9 +588,12 @@
             dx = (e - mean_e - normed * inverse * mean_ew) * lanes(rstd_in[layer, rows, :], D)
             above = xb[rows, :].astype(F32) if layer == LAYERS - 1 else xf[rows, :]
             total = above + dx
-            xf[rows, :] = total
             if layer:
+                xf[rows, :] = total
                 xb[rows, :] = total.astype(BF16)
+            else:
+                place = pl.ds(pl.multiple_of(lax.rem(i * PART, S), PART), PART)
+                masked[i * PART // S, place, :] = total.astype(BF16)
             vec_sum[:, at : at + D] += jnp.sum(product, axis=0, keepdims=True) * inverse
 
     def later(act, *where):
@@ -694,7 +700,7 @@
     if linked:
         reduce_begin(1, 3)
     project(1)
-    write_out = pltpu.make_async_copy(xf, out, local_sem.at[1])
+    write_out = pltpu.make_async_copy(masked, out, local_sem.at[1])
     write_out.start()
     if linked:
         reduce_second(1, 3)
@@ -746,7 +752,7 @@
         reduce_end(1)
         reduce_sent(1)
     back_input(0, (later(reduce_second, 0, 1), None, later(reduce_line, 0, 0), None))
-    write_in = pltpu.make_async_copy(xf, grad_in, local_sem.at[0])
+    write_in = pltpu.make_async_copy(masked, grad_in, local_sem.at[0])
     write_in.start()
     if linked:
         vec_pair(0, links.twin).start()
@@ -794,8 +800,8 @@
     results = pl.pallas_call(
         functools.partial(kernel, wide, narrow, linked),
         out_shape=(
-            jax.ShapeDtypeStruct((total, D), F32),
-            jax.ShapeDtypeStruct((total, D), F32),
+            jax.ShapeDtypeStruct((count, S, D), BF16),
+            jax.ShapeDtypeStruct((count, S, D), BF16),
             jax.ShapeDtypeStruct(mat_shape, F32 if linked else BF16),
             jax.ShapeDtypeStruct((LAYERS, VEC), F32),
             jax.ShapeDtypeStruct(half, BF16),
@@ -856,7 +862,7 @@
             mat_grads.astype(F32), axes, scatter_dimension=1, tiled=True
         )
         vec_grads = lax.psum(vec_grads, axes)
-    return (out.reshape(tokens.shape), grad_in.reshape(tokens.shape), mat_grads, vec_grads)
+    return (out.astype(F32), grad_in.astype(F32), mat_grads, vec_grads)
 
 
 def solution(mesh):

time: 156 us -> 156 us (level)
  local copies, waits for them, and re-layouts: 6.21 us -> 1.46 us
  other arithmetic: 0 us -> 4.57 us
    unnamed x10 -> x8, local copies, waits for them, and re-layouts: 6.21 us -> 1.46 us
    convert_element_type x0 -> x2, other arithmetic: none -> 4.57 us  [per_device(): return (out.astype(F32), grad_in.astype(F32), mat_grads, vec_grads)]
where the time goes in v4:
time: 156 us
  Pallas kernels  149 us (96%)
  other arithmetic  4.57 us (3%)
    pallas_call x1, Pallas kernels, per_device(): pl.pallas_call(functools.partial(kernel, wide, narrow, linked), out_shape...  149 us
    convert_element_type x2, other arithmetic, per_device(): return (out.astype(F32), grad_in.astype(F32), mat_grads, vec_grads)  4.57 us

profile of v4, /device:TPU:8, one launch (start us, length us, event | category | flops | bytes accessed | tf_op | source)
XLA Modules:
  0.0 155.9 jit_solution(12746164315568837150)
XLA Ops:
  0.6 149.2 %shard_map.84 = (bf16[2,512,512]{2,1,0:T(8,128)(2,1)}, bf16[2,512,512]{2,1,0:T(8,128)(2,1)}, f32[2,160,512]{2,1,0:T(8,128)}, f32[2,2560]{1,0:T(2,128)}, bf16[102...) custom-call(bf16[1024,512]{1,0:T(8,128)(2,1)} %bitcast.2, ...), custom_call_target="tpu_custom_call" | custom-call | tf_op jit(solution)/shard_map/pallas_call | solution.py:800
  149.9 0.0 copy-start
  149.9 0.0 copy-start.1
  149.9 0.0 copy-start.2
  149.9 3.0 %convert_element_type.6 = f32[2,512,512]{2,1,0:T(8,128)} convert(bf16[2,512,512]{2,1,0:T(8,128)(2,1)} %get-tuple-element.8) | non-fusion elementwise | flops 524288 | bytes 3145728 | tf_op jit(solution)/shard_map/convert_element_type | solution.py:865
  152.8 0.0 copy-done
  152.8 1.6 %convert_element_type.7 = f32[2,512,512]{2,1,0:T(8,128)} convert(bf16[2,512,512]{2,1,0:T(8,128)(2,1)S(1)} %copy-done) | non-fusion elementwise | flops 524288 | bytes 3145728 | tf_op jit(solution)/shard_map/convert_element_type | solution.py:865
  154.5 0.0 copy-done.1
  154.5 0.8 copy.11
  155.3 0.0 copy-done.2
  155.3 0.6 copy.12
Async XLA Ops:
  149.9 3.0 %copy-start = (bf16[2,512,512]{2,1,0:T(8,128)(2,1)S(1)}, bf16[2,512,512]{2,1,0:T(8,128)(2,1)}, u32[]{:S(2)}) copy-start(bf16[2,512,512]{2,1,0:T(8,128)(2,1)} %get-tuple-element.9) | copy-start | bytes 3145732
  149.9 4.6 %copy-start.1 = (f32[2,160,512]{2,1,0:T(8,128)S(1)}, f32[2,160,512]{2,1,0:T(8,128)}, u32[]{:S(2)}) copy-start(f32[2,160,512]{2,1,0:T(8,128)} %get-tuple-element.18) | copy-start | bytes 1966084
  149.9 5.4 %copy-start.2 = (f32[2,2560]{1,0:T(2,128)S(1)}, f32[2,2560]{1,0:T(2,128)}, u32[]{:S(2)}) copy-start(f32[2,2560]{1,0:T(2,128)} %get-tuple-element.19) | copy-start | bytes 61444
